TPU v7x, 256 devices: a whole 4x4x8 slice. The times are simulated.
256 devices in a mesh: sector: 16 (over y_lo, z), ax: 4 (over y_hi, core), rad: 4 (over x).
Axes of the slice: x: 4, y: 4 (y_hi: 2, y_lo: 2; y = y_hi * 2 + y_lo), z: 8, core: 2. Of those that a mesh axis runs over, the one named last changes fastest.
Arguments:
- mass_excess: float32 [256, 128, 512], P('sector', 'ax', 'rad'), may hold values from -0.3 to 0.3
- speed_vector: float32 [3, 256, 128, 512], P(None, 'sector', 'ax', 'rad'), may hold values from -3 to 3
- thermal_excess: float32 [256, 128, 512], P('sector', 'ax', 'rad'), may hold values from -0.5 to 0.5
- energy_release: float32 [256, 128, 512], P('sector', 'ax', 'rad'), may hold values from -8 to 8
Outputs:
- new_density: float32 [256, 128, 512], P('sector', 'ax', 'rad')
- new_velocity: float32 [3, 256, 128, 512], P(None, 'sector', 'ax', 'rad')
- new_temperature: float32 [256, 128, 512], P('sector', 'ax', 'rad')
- harmonics: float32 [128, 128, 512], P('sector', 'ax', 'rad')
All inputs are finite; a program needn't handle non-finite values.
Results may differ from a plain program's by a relative error of at most 0.00007.
Values sent between devices are 32-bit elements; how exact they have to be, the bound alone decides.
No kernel may reach another device: no remote copies, remote signals or barrier semaphores. Data moves between devices by JAX's collectives and lax.ppermute only.
A program may use at most 64 MiB of HBM per device.

v0:
```python
import math

import jax
import jax.numpy as jnp
from jax import lax
from jax.sharding import PartitionSpec as P

HARM = 128


HEAT_RATIO = 1.4
STEP_DT = 0.1
VISCOSITY = 0.1
DIFFUSIVITY = 0.1


def with_halo(block, sides, width, periodic):
    for axis, dim in sides:
        count = lax.axis_size(axis)
        forward = [(i, i + 1) for i in range(count - 1)]
        if periodic:
            forward.append((count - 1, 0))
        backward = [(target, source) for source, target in forward]
        low = lax.ppermute(
            lax.slice_in_dim(block, block.shape[dim] - width, None, axis=dim), axis, forward
        )
        high = lax.ppermute(lax.slice_in_dim(block, 0, width, axis=dim), axis, backward)
        block = jnp.concatenate([low, block, high], axis=dim)
    return block


def first_diff(padded_fields, array_axis):
    length = padded_fields.shape[array_axis] - 4

    def take(offset):
        return lax.slice_in_dim(padded_fields, offset, offset + length, axis=array_axis)

    return (8.0 * (take(3) - take(1)) - (take(4) - take(0))) / 12.0


def second_diff(padded_fields, array_axis):
    length = padded_fields.shape[array_axis] - 4

    def take(offset):
        return lax.slice_in_dim(padded_fields, offset, offset + length, axis=array_axis)

    return (16.0 * (take(3) + take(1)) - 30.0 * take(2) - (take(4) + take(0))) / 12.0


def advance(fluid_snapshot, padded_list, energy_release, spacing_theta):
    mass_excess = fluid_snapshot[0]
    speed_vector = fluid_snapshot[1:4]
    thermal_profile = fluid_snapshot[4]
    inverse = 1.0 / (1.0 + mass_excess)
    continuity = jnp.zeros_like(mass_excess)
    convective_transport = jnp.zeros_like(fluid_snapshot[1:5])
    diffusion_operator = jnp.zeros_like(fluid_snapshot[1:5])
    spreading_sum = jnp.zeros_like(mass_excess)
    pressure_terms = []
    for direction in range(3):
        padded_fields = padded_list[direction]
        spacing = spacing_theta if direction == 0 else 1.0
        slopes = first_diff(padded_fields, direction + 1) / spacing
        curves = second_diff(padded_fields[1:5], direction + 1) / (spacing * spacing)
        mass_flux = (1.0 + padded_fields[0]) * padded_fields[1 + direction]
        pressure = (1.0 + padded_fields[0]) * (1.0 + padded_fields[4]) / HEAT_RATIO
        continuity = continuity - first_diff(mass_flux, direction) / spacing
        pressure_terms.append(first_diff(pressure, direction) / spacing)
        convective_transport = convective_transport + speed_vector[direction][None] * slopes[1:5]
        diffusion_operator = diffusion_operator + curves
        spreading_sum = spreading_sum + slopes[1 + direction]
    velocity_rate = (
        -convective_transport[0:3]
        - jnp.stack(pressure_terms) * inverse[None]
        + VISCOSITY * diffusion_operator[0:3]
    )
    warming_derivative = (
        -convective_transport[3]
        - (HEAT_RATIO - 1.0) * (1.0 + thermal_profile) * spreading_sum
        + DIFFUSIVITY * diffusion_operator[3]
        + energy_release
    )
    rates = jnp.concatenate([continuity[None], velocity_rate, warming_derivative[None]], axis=0)
    return fluid_snapshot + STEP_DT * rates


def harmonic_basis(rows, thetas, ntheta, harm):
    half = harm // 2
    orders = jnp.where(rows <= half, rows, rows - half)
    use_sine = rows > half
    phase = orders[:, None] * thetas[None, :] % ntheta
    angle = phase.astype(jnp.float32) * (2.0 * math.pi / ntheta)
    values = jnp.where(use_sine[:, None], jnp.sin(angle), jnp.cos(angle))
    return values / math.sqrt(ntheta)


def per_device(mass_excess, speed_vector, thermal_excess, energy_release):
    cells_theta, cells_axial, cells_radial = mass_excess.shape
    sectors = lax.axis_size("sector")
    ntheta = cells_theta * sectors
    nradial = cells_radial * lax.axis_size("rad")
    fluid_snapshot = jnp.concatenate(
        [mass_excess[None], speed_vector, thermal_excess[None]], axis=0
    )
    theta_pad = with_halo(fluid_snapshot, (("sector", 1),), 2, True)
    plane = with_halo(fluid_snapshot, (("ax", 2), ("rad", 3)), 2, False)
    axial_pad = plane[:, :, :, 2:-2]
    radial_pad = plane[:, :, 2:-2, :]
    radial_index = (
        lax.axis_index("rad") * cells_radial + jnp.arange(cells_radial, dtype=jnp.int32)
    ).astype(jnp.float32)
    spacing_theta = (0.5 + (radial_index + 0.5) / nradial).reshape(1, 1, cells_radial)
    fresh = advance(
        fluid_snapshot, [theta_pad, axial_pad, radial_pad], energy_release, spacing_theta
    )
    new_temper = fresh[4]
    flat_temper = new_temper.reshape(cells_theta, cells_axial * cells_radial)
    thetas = lax.axis_index("sector") * cells_theta + jnp.arange(cells_theta, dtype=jnp.int32)
    rows = jnp.arange(lax.axis_size("sector") * (HARM // sectors), dtype=jnp.int32)
    basis = harmonic_basis(rows, thetas, ntheta, HARM)
    terms = jnp.dot(
        basis, flat_temper, precision=lax.Precision.HIGHEST, preferred_element_type=jnp.float32
    )
    coeffs = lax.psum_scatter(
        terms.reshape(lax.axis_size("sector") * (HARM // sectors), cells_axial, cells_radial),
        "sector",
        scatter_dimension=0,
        tiled=True,
    )
    return (fresh[0], fresh[1:4], new_temper, coeffs)


def solution(mesh):
    return jax.shard_map(
        per_device,
        mesh=mesh,
        in_specs=(
            P("sector", "ax", "rad"),
            P(None, "sector", "ax", "rad"),
            P("sector", "ax", "rad"),
            P("sector", "ax", "rad"),
        ),
        out_specs=(
            P("sector", "ax", "rad"),
            P(None, "sector", "ax", "rad"),
            P("sector", "ax", "rad"),
            P("sector", "ax", "rad"),
        ),
        check_vma=False,
    )
```

profile of v0, /device:TPU:2, one launch (start us, length us, event | category | flops | bytes accessed | tf_op | source)
XLA Modules:
  0.0 148.6 jit_solution(7056606973969617093)
XLA Ops:
  7.2 1.4 pad_maximum_fusion.4
  8.7 1.4 collective-permute-start.3
  10.2 3.2 %collective-permute-start.2 = (f32[5,16,2,128]{3,1,2,0:T(8,128)S(1)}, f32[5,16,2,128]{3,1,2,0:T(8,128)S(1)}, u32[]{:S(2)}, u32[]{:S(2)}) collective-permute-start(f32[5,16,2,128]{3,1,2,0:T(8,128)S(1)} %copy.165), channel_id=1, source_target_pairs={{0,4},{4,8},{8,12},{1,5},{5,9},{9,13},{2,6},{6,10},{10,14},{3,7},{... | collective-permute-start | bytes 245768 | tf_op jit(solution)/shard_map/ppermute | solution.py:24
  14.1 6.9 %collective-permute-start.1 = (f32[5,2,32,128]{3,2,1,0:T(8,128)}, f32[5,2,32,128]{3,2,1,0:T(8,128)}, u32[]{:S(2)}, u32[]{:S(2)}) collective-permute-start(f32[5,2,32,128]{3,2,1,0:T(8,128)} %get-tuple-element.47), channel_id=1, source_target_pairs={{16,0},{32,16},{48,32},{64,48},{80,64},{96,80},{112,96},{128,112},... | collective-permute-start | bytes 491528 | tf_op jit(solution)/shard_map/ppermute | solution.py:27
  21.8 0.9 slice_bitcast_fusion.3
  23.1 1.7 %pad_maximum_fusion.2 = (f32[5,16,34,128]{3,2,1,0:T(8,128)S(1)}, f32[5,16,34,128]{3,2,1,0:T(8,128)}) fusion(f32[5,16,2,128]{3,2,1,0:T(2,128)S(1)} %copy.154, f32[1,16,32,128]{3,2,1,0:T(8,128)S(1)} %bitcast.83, f32[3,16,32,128]{3,2,1,0:T(8,128)S(1)} %copy-done, f32[1,16,32,128]{3,2,1,0:T(8,128)S(1)} %bitcast.94, f32[5,16,2,128]{3,2,1,0:T(2,128)S(1)} %copy.153), kind=kLoop, calls=%fused_computation.3 | loop fusion | flops 2088960 | bytes 4259840 | tf_op jit(solution)/shard_map/concatenate | solution.py:28
  24.8 2.3 %fusion.108 = (f32[5,16,36,2]{3,2,1,0:T(8,128)}, f32[5,16,36,2]{3,2,1,0:T(8,128)}) fusion(f32[5,16,36,128]{3,2,1,0:T(8,128)S(1)} %pad_maximum_fusion.1), kind=kLoop, calls=%fused_computation.190 | loop fusion | bytes 92160 | tf_op jit(solution)/shard_map/slice | solution.py:27
  27.1 2.7 %copy.156 = f32[5,16,36,2]{2,1,3,0:T(8,128)} copy(f32[5,16,36,2]{3,2,1,0:T(8,128)} %get-tuple-element.38) | data formatting | bytes 46080 | tf_op jit(solution)/shard_map/slice | solution.py:27
  29.8 2.1 %copy.155 = f32[5,16,36,2]{2,1,3,0:T(8,128)S(1)} copy(f32[5,16,36,2]{3,2,1,0:T(8,128)} %get-tuple-element.39) | data formatting | bytes 46080 | tf_op jit(solution)/shard_map/slice | solution.py:25
  31.9 3.4 %collective-permute-start.4 = (f32[5,16,36,2]{2,1,3,0:T(8,128)S(1)}, f32[5,16,36,2]{2,1,3,0:T(8,128)}, u32[]{:S(2)}, u32[]{:S(2)}) collective-permute-start(f32[5,16,36,2]{2,1,3,0:T(8,128)S(1)} %copy.155), channel_id=1, source_target_pairs={{0,1},{1,2},{2,3},{4,5},{5,6},{6,7},{8,9},{9,10},{10,11},{12,13},{... | collective-permute-start | bytes 69128 | tf_op jit(solution)/shard_map/ppermute | solution.py:24
  35.3 3.2 %collective-permute-start.5 = (f32[5,16,36,2]{2,1,3,0:T(8,128)}, f32[5,16,36,2]{2,1,3,0:T(8,128)}, u32[]{:S(2)}, u32[]{:S(2)}) collective-permute-start(f32[5,16,36,2]{2,1,3,0:T(8,128)} %copy.156), channel_id=1, source_target_pairs={{1,0},{2,1},{3,2},{5,4},{6,5},{7,6},{9,8},{10,9},{11,10},{13,12},{... | collective-permute-start | bytes 69128 | tf_op jit(solution)/shard_map/ppermute | solution.py:27
  38.6 3.5 %fusion.4 = f32[5,16,32,128]{3,2,1,0:T(8,128)} fusion(f32[5,16,34,128]{3,2,1,0:T(8,128)} %get-tuple-element.50, f32[5,16,34,128]{3,2,1,0:T(8,128)S(1)} %get-tuple-element.49), kind=kLoop, calls=%fused_computation.14 | loop fusion | flops 1638400 | bytes 6553600 | tf_op jit(solution)/shard_map/div | solution.py:38
  42.9 1.6 %copy.158 = f32[5,16,36,2]{3,2,1,0:T(8,128)S(1)} copy(f32[5,16,36,2]{2,1,3,0:T(8,128)} %collective-permute-done.5) | data formatting | bytes 46080 | tf_op jit(solution)/shard_map/ppermute | solution.py:27
  44.5 2.7 %copy.157 = f32[5,16,36,2]{3,2,1,0:T(8,128)} copy(f32[5,16,36,2]{2,1,3,0:T(8,128)} %collective-permute-done.4) | data formatting | bytes 46080 | tf_op jit(solution)/shard_map/ppermute | solution.py:24
  47.2 1.7 %fusion.33 = f32[16,32,132]{2,1,0:T(8,128)S(1)} fusion(f32[5,16,36,2]{3,2,1,0:T(8,128)S(1)} %copy.158, f32[5,16,36,2]{3,2,1,0:T(8,128)} %copy.157, f32[5,16,2,128]{3,2,1,0:T(2,128)S(1)} %copy.154, f32[5,16,2,128]{3,2,1,0:T(2,128)S(1)} %copy.153, f32[1,16,32,128]{3,2,1,0:T(8,128)S(1)} %bitcast.84, f32[3,16,32,128]{3,2,1,0:T(8,128)S(1)} %copy-done, ...), kind=kLoop, calls=%fused_computation.62 | loop fusion | flops 1081344 | bytes 1790976 | tf_op jit(solution)/shard_map/div | solution.py:66
  49.0 2.4 %pad_maximum_fusion = (f32[5,16,36,130]{3,2,1,0:T(8,128)S(1)}, f32[5,16,36,130]{3,2,1,0:T(8,128)S(1)}) fusion(f32[5,16,36,2]{3,2,1,0:T(8,128)S(1)} %copy.158, f32[5,16,2,128]{3,2,1,0:T(2,128)S(1)} %copy.154, f32[1,16,32,128]{3,2,1,0:T(8,128)S(1)} %bitcast.85, f32[3,16,32,128]{3,2,1,0:T(8,128)S(1)} %copy-done, f32[1,16,32,128]{3,2,1,0:T(8,128)S(1)} %bitcast.96, ...), kind=kLoop, calls=%fused_computation | loop fusion | flops 3744000 | bytes 4515840 | tf_op jit(solution)/shard_map/concatenate | solution.py:28
  51.4 1.1 fusion.1
  53.4 1.4 pad_maximum_fusion.3
  55.1 1.1 copy-done.5
  56.7 1.8 %fusion.13 = f32[4,16,32,128]{3,2,1,0:T(8,128)S(1)} fusion(f32[5,16,36,130]{3,2,1,0:T(8,128)S(1)} %get-tuple-element.41, f32[5,16,36,130]{3,2,1,0:T(8,128)S(1)} %get-tuple-element.40, f32[5,16,34,128]{3,2,1,0:T(8,128)S(1)} %copy-done.6, f32[5,16,34,128]{3,2,1,0:T(8,128)S(1)} %copy-done.5, f32[5,18,32,128]{3,2,1,0:T(8,128)S(1)} %get-tuple-element.46, ...), kind=kLoop, calls=%fused_computation.29 | loop fusion | flops 6029312 | bytes 14680576 | tf_op jit(solution)/shard_map/add | solution.py:70
  63.9 3.3 %fusion.42 = f32[128,32,128]{2,0,1:T(8,128)} fusion(s32[16]{0:T(128)S(1)} %iota_add_fusion, s32[128]{0:T(128)S(1)} %compare_select_fusion, pred[128]{0:T(512)(128)(4,1)S(1)} %iota_compare_fusion, f32[2,8,32,128]{3,2,1,0:T(8,128)S(1)} %bitcast.102), kind=kOutput, calls=%fused_computation.94 | convolution fusion | flops 100696064 | bytes 2360000 | tf_op jit(solution)/shard_map/dot_general | solution.py:121
  67.2 0.9 slice.456
  68.1 72.0 %reduce-scatter.2.cloned.1.call-done = f32[8,32,128]{2,0,1:T(8,128)} async-done(((f32[128,32,128]{2,0,1:T(8,128)}), f32[8,32,128]{2,0,1:T(8,128)}) %reduce-scatter.2.cloned.1.call-update) | async-done | bytes 131088 | tf_op jit(solution)/shard_map/reduce_scatter | solution.py:124
  140.1 1.6 %copy.164 = f32[8,32,128]{2,1,0:T(8,128)} copy(f32[8,32,128]{2,0,1:T(8,128)} %reduce-scatter.2.cloned.1.call-done) | data formatting | bytes 262144
  (64 shorter events, 9.9 us)
Async XLA Ops:
  7.2 133.0 %reduce-scatter.2.cloned.1.call-start = ((), (), s32[]{:S(2)}) async-start(), calls=%async_computation.1 | async-start | bytes 2228224 | tf_op jit(solution)/shard_map/reduce_scatter | solution.py:124
  7.2 13.8 %copy-start.2 = (f32[16,32,128]{2,1,0:T(8,128)S(1)}, f32[16,32,128]{2,1,0:T(8,128)}, u32[]{:S(2)}) copy-start(f32[16,32,128]{2,1,0:T(8,128)} %param.4) | copy-start | bytes 786436
  8.6 13.1 %copy-start = (f32[3,16,32,128]{3,2,1,0:T(8,128)S(1)}, f32[3,16,32,128]{3,2,1,0:T(8,128)}, u32[]{:S(2)}) copy-start(f32[3,16,32,128]{3,2,1,0:T(8,128)} %param.5) | copy-start | bytes 2359300
  8.7 14.0 %collective-permute-start.3 = (f32[5,16,2,128]{3,1,2,0:T(8,128)S(1)}, f32[5,16,2,128]{3,1,2,0:T(8,128)S(1)}, u32[]{:S(2)}, u32[]{:S(2)}) collective-permute-start(f32[5,16,2,128]{3,1,2,0:T(8,128)S(1)} %copy.166), channel_id=1, source_target_pairs={{4,0},{8,4},{12,8},{5,1},{9,5},{13,9},{6,2},{10,6},{14,10},{7,3},{... | collective-permute-start | bytes 245768 | tf_op jit(solution)/shard_map/ppermute | solution.py:27
  10.2 12.6 %copy-start.1 = (f32[16,32,128]{2,1,0:T(8,128)S(1)}, f32[16,32,128]{2,1,0:T(8,128)}, u32[]{:S(2)}) copy-start(f32[16,32,128]{2,1,0:T(8,128)} %param.6) | copy-start | bytes 786436
  10.2 12.6 %collective-permute-start.2 = (f32[5,16,2,128]{3,1,2,0:T(8,128)S(1)}, f32[5,16,2,128]{3,1,2,0:T(8,128)S(1)}, u32[]{:S(2)}, u32[]{:S(2)}) collective-permute-start(f32[5,16,2,128]{3,1,2,0:T(8,128)S(1)} %copy.165), channel_id=1, source_target_pairs={{0,4},{4,8},{8,12},{1,5},{5,9},{9,13},{2,6},{6,10},{10,14},{3,7},{... | collective-permute-start | bytes 245768 | tf_op jit(solution)/shard_map/ppermute | solution.py:24
  14.1 39.3 %collective-permute-start.1 = (f32[5,2,32,128]{3,2,1,0:T(8,128)}, f32[5,2,32,128]{3,2,1,0:T(8,128)}, u32[]{:S(2)}, u32[]{:S(2)}) collective-permute-start(f32[5,2,32,128]{3,2,1,0:T(8,128)} %get-tuple-element.47), channel_id=1, source_target_pairs={{16,0},{32,16},{48,32},{64,48},{80,64},{96,80},{112,96},{128,112},... | collective-permute-start | bytes 491528 | tf_op jit(solution)/shard_map/ppermute | solution.py:27
  21.0 32.4 %collective-permute-start = (f32[5,2,32,128]{3,2,1,0:T(8,128)}, f32[5,2,32,128]{3,2,1,0:T(8,128)}, u32[]{:S(2)}, u32[]{:S(2)}) collective-permute-start(f32[5,2,32,128]{3,2,1,0:T(8,128)} %get-tuple-element.48), channel_id=1, source_target_pairs={{0,16},{16,32},{32,48},{48,64},{64,80},{80,96},{96,112},{112,128},... | collective-permute-start | bytes 491528 | tf_op jit(solution)/shard_map/ppermute | solution.py:24
  23.1 1.7 %copy-start.7 = (f32[5,16,36,128]{3,2,1,0:T(8,128)}, f32[5,16,36,128]{3,2,1,0:T(8,128)S(1)}, u32[]{:S(2)}) copy-start(f32[5,16,36,128]{3,2,1,0:T(8,128)S(1)} %pad_maximum_fusion.1) | copy-start | bytes 4423684
  24.8 13.7 %copy-start.4 = (f32[5,16,34,128]{3,2,1,0:T(8,128)}, f32[5,16,34,128]{3,2,1,0:T(8,128)S(1)}, u32[]{:S(2)}) copy-start(f32[5,16,34,128]{3,2,1,0:T(8,128)S(1)} %get-tuple-element.49) | copy-start | bytes 4177924
  31.9 12.6 %collective-permute-start.4 = (f32[5,16,36,2]{2,1,3,0:T(8,128)S(1)}, f32[5,16,36,2]{2,1,3,0:T(8,128)}, u32[]{:S(2)}, u32[]{:S(2)}) collective-permute-start(f32[5,16,36,2]{2,1,3,0:T(8,128)S(1)} %copy.155), channel_id=1, source_target_pairs={{0,1},{1,2},{2,3},{4,5},{5,6},{6,7},{8,9},{9,10},{10,11},{12,13},{... | collective-permute-start | bytes 69128 | tf_op jit(solution)/shard_map/ppermute | solution.py:24
  35.3 7.6 %collective-permute-start.5 = (f32[5,16,36,2]{2,1,3,0:T(8,128)}, f32[5,16,36,2]{2,1,3,0:T(8,128)}, u32[]{:S(2)}, u32[]{:S(2)}) collective-permute-start(f32[5,16,36,2]{2,1,3,0:T(8,128)} %copy.156), channel_id=1, source_target_pairs={{1,0},{2,1},{3,2},{5,4},{6,5},{7,6},{9,8},{10,9},{11,10},{13,12},{... | collective-permute-start | bytes 69128 | tf_op jit(solution)/shard_map/ppermute | solution.py:27
  38.6 3.5 %copy-start.8 = (f32[5,16,36,128]{3,2,1,0:T(8,128)S(1)}, f32[5,16,36,128]{3,2,1,0:T(8,128)}, u32[]{:S(2)}) copy-start(f32[5,16,36,128]{3,2,1,0:T(8,128)} %copy-done.7) | copy-start | bytes 4423684
  47.2 1.7 %copy-start.3 = (f32[5,16,36,2]{3,2,1,0:T(8,128)S(1)}, f32[5,16,36,2]{3,2,1,0:T(8,128)}, u32[]{:S(2)}) copy-start(f32[5,16,36,2]{3,2,1,0:T(8,128)} %copy.157) | copy-start | bytes 69124
  51.4 1.1 copy-start.9
  54.8 1.4 copy-start.5
  54.8 1.9 %copy-start.6 = (f32[5,16,34,128]{3,2,1,0:T(8,128)S(1)}, f32[5,16,34,128]{3,2,1,0:T(8,128)}, u32[]{:S(2)}) copy-start(f32[5,16,34,128]{3,2,1,0:T(8,128)} %get-tuple-element.50) | copy-start | bytes 4177924
  56.7 1.8 %copy-start.10 = (f32[5,16,32,128]{3,2,1,0:T(8,128)S(1)}, f32[5,16,32,128]{3,2,1,0:T(8,128)}, u32[]{:S(2)}) copy-start(f32[5,16,32,128]{3,2,1,0:T(8,128)} %fusion.4) | copy-start | bytes 3932164
  56.7 1.8 %copy-start.11 = (f32[16,32,128]{2,1,0:T(8,128)S(1)}, f32[16,32,128]{2,1,0:T(8,128)}, u32[]{:S(2)}) copy-start(f32[16,32,128]{2,1,0:T(8,128)} %get-tuple-element.53) | copy-start | bytes 786436
  56.7 1.8 %copy-start.12 = (f32[16,32,128]{2,1,0:T(8,128)S(1)}, f32[16,32,128]{2,1,0:T(8,128)}, u32[]{:S(2)}) copy-start(f32[16,32,128]{2,1,0:T(8,128)} %get-tuple-element.54) | copy-start | bytes 786436
  56.7 1.8 %copy-start.13 = (f32[16,32,128]{2,1,0:T(8,128)S(1)}, f32[16,32,128]{2,1,0:T(8,128)}, u32[]{:S(2)}) copy-start(f32[16,32,128]{2,1,0:T(8,128)} %get-tuple-element.55) | copy-start | bytes 786436
  58.5 1.0 copy-start.15
  61.4 1.0 copy-start.14
Sparse Core Ops, SparseCore 0:
  67.3 72.7 reduce-scatter.1
where the time goes:
time: 149 us
  waiting for transfers between devices  72 us (48%)
  other arithmetic  21.4 us (14%)
  local copies, waits for them, and re-layouts  19.3 us (13%)
  starting transfers between devices  18.1 us (12%)
  between operations  14.4 us (10%)
  matrix products  3.32 us (2%)
    reduce_scatter x1, waiting for transfers between devices, per_device(): lax.psum_scatter(terms.reshape(lax.axis_size('sector') * (HARM // sectors...  72 us
    ppermute x3, starting transfers between devices, with_halo(): lax.ppermute(lax.slice_in_dim(block, 0, width, axis=dim), axis, backward)  11.5 us
    ppermute x3, starting transfers between devices, with_halo(): lax.ppermute(lax.slice_in_dim(block, block.shape[dim] - width, None, axis...  6.57 us
    slice x3, local copies, waits for them, and re-layouts, with_halo(): lax.slice_in_dim(block, 0, width, axis=dim)  5.76 us
    concatenate x4, other arithmetic, with_halo(): block = jnp.concatenate([low, block, high], axis=dim)  5.75 us
    div x2, other arithmetic, first_diff(): return (8.0 * (take(3) - take(1)) - (take(4) - take(0))) / 12.0  4.6 us
    unnamed x35, local copies, waits for them, and re-layouts  4.3 us
    dot_general x1, matrix products, per_device(): jnp.dot(basis, flat_temper, precision=lax.Precision.HIGHEST, preferred_el...  3.32 us
  transfers between devices with their start and end apart: 7, of which 1 were waited for; matrix products, arithmetic and copies ran while one was open for 18% of the time, Pallas kernels for 0%

commit v1 on v0

v1 whole, which is shorter than its diff:
```python
import math

import jax
import jax.numpy as jnp
import numpy as np
from jax import lax
from jax.experimental import pallas as pl
from jax.experimental.pallas import tpu as pltpu
from jax.sharding import PartitionSpec as P

HARM = 128
HEAT_RATIO = 1.4
STEP_DT = 0.1
VISCOSITY = 0.1
DIFFUSIVITY = 0.1
VMEM_LIMIT = 40 * 1024 * 1024


def basis_table(ntheta):
    half = HARM // 2
    rows = np.arange(HARM)
    orders = np.where(rows <= half, rows, rows - half)
    phase = orders[:, None] * np.arange(ntheta)[None, :] % ntheta
    angle = phase * (2.0 * math.pi / ntheta)
    values = np.where((rows > half)[:, None], np.sin(angle), np.cos(angle))
    return (values / math.sqrt(ntheta)).astype(np.float32)


def edges_kernel(rho, vel, temp, s_lo, s_hi, a_lo, a_hi, r_pack):
    nt, na, nr = rho.shape
    fields = [rho, vel.at[0], vel.at[1], vel.at[2], temp]
    lane = lax.broadcasted_iota(jnp.int32, (na, nr), 1)
    for f, ref in enumerate(fields):
        s_lo[f] = ref[0:2]
        s_hi[f] = ref[nt - 2 : nt]
        packed = jnp.zeros((na, nr), jnp.float32)
        for t in range(nt):
            for side in range(2):
                a_lo[f, side, pl.ds(t, 1), :] = ref[t, pl.ds(side, 1), :]
                a_hi[f, side, pl.ds(t, 1), :] = ref[t, pl.ds(na - 2 + side, 1), :]
            x = ref[t]
            turned = pltpu.roll(x, 8 * t, 1) if t else x
            near = (lane + 2 - 8 * t) % nr < 4
            packed = jnp.where(near, turned, packed)
        r_pack[f] = packed


def stencil_kernel(
    rho, vel, temp, heat, s_lo, s_hi, a_lo, a_hi, r_left, r_right,
    new_rho, new_vel, new_temp, cells,
    pad, flux_t, flux_a, flux_r, press, r_halo,
):
    nt, na, nr = rho.shape
    ax, rad = lax.axis_index("ax"), lax.axis_index("rad")
    nax, nrad = lax.axis_size("ax"), lax.axis_size("rad")
    keep_al = jnp.where(ax > 0, 1.0, 0.0)
    keep_ah = jnp.where(ax < nax - 1, 1.0, 0.0)
    keep_rl = jnp.where(rad > 0, 1.0, 0.0)
    keep_rh = jnp.where(rad < nrad - 1, 1.0, 0.0)
    fields = [rho, vel.at[0], vel.at[1], vel.at[2], temp]
    lane = lax.broadcasted_iota(jnp.int32, (na, nr), 1)
    mod8 = lane % 8
    for f, ref in enumerate(fields):
        pad[f, 0:2, 8 : 8 + na] = s_lo[f]
        pad[f, nt + 2 : nt + 4, 8 : 8 + na] = s_hi[f]
        for t in range(nt):
            pad[f, t + 2, 8 : 8 + na] = ref[t]
            for side in range(2):
                pad[f, t + 2, 6 + side : 7 + side] = a_lo[f, side, pl.ds(t, 1), :] * keep_al
                pad[f, t + 2, 8 + na + side : 9 + na + side] = (
                    a_hi[f, side, pl.ds(t, 1), :] * keep_ah
                )
        r_halo[f] = jnp.where(mod8 < 2, r_right[f] * keep_rh, r_left[f] * keep_rl)
    r_halo[5] = (1.0 + r_halo[0]) * r_halo[3]
    r_halo[6] = (1.0 + r_halo[0]) * (1.0 + r_halo[4])

    def products(t, carry):
        mass = 1.0 + pad[0, t]
        flux_t[t] = mass * pad[1, t]
        press[t] = mass * (1.0 + pad[4, t])
        return carry

    lax.fori_loop(0, nt + 4, products, 0)

    def products_in(t, carry):
        mass = 1.0 + pad[0, t + 2]
        flux_a[t] = mass * pad[2, t + 2]
        flux_r[t] = mass[8 : 8 + na] * pad[3, t + 2, 8 : 8 + na]
        return carry

    lax.fori_loop(0, nt, products_in, 0)

    sub = 8
    lane8 = lax.broadcasted_iota(jnp.int32, (sub, nr), 1)
    radius = (rad * nr + lane8).astype(jnp.float32)
    h = 0.5 + (radius + 0.5) / (nr * nrad)
    inv12h = 1.0 / (12.0 * h)
    inv12 = 1.0 / 12.0
    gt = VISCOSITY / (12.0 * h * h)
    g = VISCOSITY / 12.0
    first, last = lane8 == 0, lane8 == nr - 1
    first2, last2 = lane8 < 2, lane8 >= nr - 2

    def step(t, carry):
        turn = (nr - 8 * t) % nr
        halos = [pltpu.roll(r_halo[q], turn, 1) for q in range(1, 7)]
        for j in range(na // sub):
            lo = 8 + j * sub
            rows = slice(lo, lo + sub)

            def lanes(mid, halo):
                ht = halo[j * sub : (j + 1) * sub]
                return [
                    pltpu.roll(jnp.where(last2, ht, mid), 2, 1),
                    pltpu.roll(jnp.where(last, ht, mid), 1, 1),
                    pltpu.roll(jnp.where(first, ht, mid), nr - 1, 1),
                    pltpu.roll(jnp.where(first2, ht, mid), nr - 2, 1),
                ]

            def around(ref, mid, halo):
                return (
                    [ref[t + 2 + d, rows] for d in (-2, -1, 1, 2)],
                    [ref[t + 2, lo + d : lo + d + sub] for d in (-2, -1, 1, 2)],
                    lanes(mid, halo),
                )

            def d1(s):
                return 8.0 * (s[2] - s[1]) - (s[3] - s[0])

            r0 = pad[0, t + 2, rows]
            u = [pad[1 + c, t + 2, rows] for c in range(3)]
            w = [u[0] * inv12h, u[1] * inv12, u[2] * inv12]
            fresh = []
            div = None
            for c in range(1, 5):
                mid = u[c - 1] if c < 4 else pad[4, t + 2, rows]
                st, sa, sr = around(pad.at[c], mid, halos[c - 1])
                slopes = [d1(st), d1(sa), d1(sr)]
                if c < 4:
                    part = slopes[c - 1] * (inv12h if c == 1 else inv12)
                    div = part if div is None else div + part
                ring1 = (sa[1] + sa[2]) + (sr[1] + sr[2])
                ring2 = (sa[0] + sa[3]) + (sr[0] + sr[3])
                curve_t = 16.0 * (st[1] + st[2]) - 30.0 * mid - (st[0] + st[3])
                curve = 16.0 * ring1 - 60.0 * mid - ring2
                rate = gt * curve_t + g * curve - (
                    w[0] * slopes[0] + w[1] * slopes[1] + w[2] * slopes[2]
                )
                fresh.append((mid, rate))
            mid, rate = fresh[3]
            rate = rate - (HEAT_RATIO - 1.0) * (1.0 + mid) * div + heat[t, j * sub : (j + 1) * sub]
            value = mid + STEP_DT * rate
            new_temp[t, j * sub : (j + 1) * sub] = value

            pmid = press[t + 2, rows]
            pt, pa, pr = around(press, pmid, halos[5])
            scale = 1.0 / (HEAT_RATIO * (1.0 + r0))
            grads = [d1(pt) * inv12h, d1(pa) * inv12, d1(pr) * inv12]
            for c in range(3):
                mid, rate = fresh[c]
                new_vel[c, t, j * sub : (j + 1) * sub] = mid + STEP_DT * (rate - grads[c] * scale)

            ft = [flux_t[t + 2 + d, rows] for d in (-2, -1, 1, 2)]
            fa = [flux_a[t, lo + d : lo + d + sub] for d in (-2, -1, 1, 2)]
            fr = lanes(flux_r[t, j * sub : (j + 1) * sub], halos[4])
            loss = d1(ft) * inv12h + (d1(fa) + d1(fr)) * inv12
            new_rho[t, j * sub : (j + 1) * sub] = r0 - STEP_DT * loss
        return carry

    lax.fori_loop(0, nt, step, 0)
    flat = new_temp.reshape(nt * na, nr)
    for a in range(na):
        cells[a] = flat[pl.ds(a, nt, stride=na), :]


def harmonics_kernel(table, spread, out):
    sectors, parts, nt, nr = spread.shape
    for p in range(parts):
        x = spread[:, p].reshape(sectors * nt, nr)
        y = jnp.dot(
            table[...], x, precision=lax.Precision.HIGHEST, preferred_element_type=jnp.float32
        )
        out[:, p] = y.reshape(sectors, HARM // sectors, nr)


def gather_kernel(parts, out):
    cells, rows, nr = parts.shape
    flat = parts.reshape(cells * rows, nr)
    for k in range(rows):
        out[k] = flat[pl.ds(k, cells, stride=rows), :]


def per_device(table, mass_excess, speed_vector, thermal_excess, energy_release):
    nt, na, nr = mass_excess.shape
    f32 = jnp.float32
    params = pltpu.CompilerParams(vmem_limit_bytes=VMEM_LIMIT)
    sds = jax.ShapeDtypeStruct
    s_lo, s_hi, a_lo, a_hi, r_pack = pl.pallas_call(
        edges_kernel,
        out_shape=(
            sds((5, 2, na, nr), f32),
            sds((5, 2, na, nr), f32),
            sds((5, 2, nt, nr), f32),
            sds((5, 2, nt, nr), f32),
            sds((5, na, nr), f32),
        ),
        compiler_params=params,
        name="edges",
    )(mass_excess, speed_vector, thermal_excess)

    def ring(axis, up):
        count = lax.axis_size(axis)
        return [(i, (i + (1 if up else -1)) % count) for i in range(count)]

    t_lo = lax.ppermute(s_hi, "sector", ring("sector", True))
    t_hi = lax.ppermute(s_lo, "sector", ring("sector", False))
    x_lo = lax.ppermute(a_hi, "ax", ring("ax", True))
    x_hi = lax.ppermute(a_lo, "ax", ring("ax", False))
    r_left = lax.ppermute(r_pack, "rad", ring("rad", True))
    r_right = lax.ppermute(r_pack, "rad", ring("rad", False))
    new_rho, new_vel, new_temp, cells = pl.pallas_call(
        stencil_kernel,
        out_shape=(
            sds((nt, na, nr), f32),
            sds((3, nt, na, nr), f32),
            sds((nt, na, nr), f32),
            sds((na, nt, nr), f32),
        ),
        scratch_shapes=[
            pltpu.VMEM((5, nt + 4, na + 16, nr), f32),
            pltpu.VMEM((nt + 4, na + 16, nr), f32),
            pltpu.VMEM((nt, na + 16, nr), f32),
            pltpu.VMEM((nt, na, nr), f32),
            pltpu.VMEM((nt + 4, na + 16, nr), f32),
            pltpu.VMEM((7, na, nr), f32),
        ],
        compiler_params=params,
        name="stencil",
    )(
        mass_excess, speed_vector, thermal_excess, energy_release,
        t_lo, t_hi, x_lo, x_hi, r_left, r_right,
    )
    sectors = lax.axis_size("sector")
    rows = HARM // sectors
    share = na // sectors
    spread = lax.all_to_all(
        cells.reshape(sectors, share, nt, nr), "sector", 0, 0, tiled=True
    )
    terms = pl.pallas_call(
        harmonics_kernel,
        out_shape=sds((sectors, share, rows, nr), f32),
        compiler_params=params,
        name="harmonics",
    )(table, spread)
    terms = lax.all_to_all(terms, "sector", 0, 0, tiled=True)
    coeffs = pl.pallas_call(
        gather_kernel,
        out_shape=sds((rows, na, nr), f32),
        compiler_params=params,
        name="gather",
    )(terms.reshape(na, rows, nr))
    return (new_rho, new_vel, new_temp, coeffs)


def solution(mesh):
    cell = P("sector", "ax", "rad")
    vector = P(None, "sector", "ax", "rad")

    def run(mass_excess, speed_vector, thermal_excess, energy_release):
        table = jnp.asarray(basis_table(mass_excess.shape[0]))
        return jax.shard_map(
            per_device,
            mesh=mesh,
            in_specs=(P(), cell, vector, cell, cell),
            out_specs=(cell, vector, cell, cell),
            check_vma=False,
        )(table, mass_excess, speed_vector, thermal_excess, energy_release)

    return run
```

time: 149 us -> 56.4 us (0.38)
  the two profiles are of different devices: /device:TPU:2 before, /device:TPU:16 now
where the time goes in v1:
time: 56.4 us; the launch traced here: 56.1 us
  blocking collectives  27.8 us (49%)
  starting transfers between devices  11.8 us (21%)
  Pallas kernels  7.2 us (13%)
  waiting for transfers between devices  5.65 us (10%)
  local copies, waits for them, and re-layouts  3.03 us (5%)
  between operations  0.68 us (1%)
    all_to_all x1, blocking collectives, per_device(): lax.all_to_all(cells.reshape(sectors, share, nt, nr), 'sector', 0, 0, til...  15.1 us
    all_to_all x1, blocking collectives, per_device(): terms = lax.all_to_all(terms, 'sector', 0, 0, tiled=True)  12.7 us
    pallas_call x1, Pallas kernels, per_device(): pl.pallas_call(stencil_kernel, out_shape=(sds((nt, na, nr), f32), sds((3,...  5.71 us
    ppermute x1, starting transfers between devices, per_device(): t_hi = lax.ppermute(s_lo, 'sector', ring('sector', False))  4.73 us
    ppermute x1, waiting for transfers between devices, per_device(): r_left = lax.ppermute(r_pack, 'rad', ring('rad', True))  3.6 us
    unnamed x10, local copies, waits for them, and re-layouts  3.03 us
    ppermute x1, starting transfers between devices, per_device(): r_right = lax.ppermute(r_pack, 'rad', ring('rad', False))  2.76 us
    ppermute x1, starting transfers between devices, per_device(): x_hi = lax.ppermute(a_lo, 'ax', ring('ax', False))  2.19 us
  transfers between devices with their start and end apart: 6, of which 2 were waited for; matrix products, arithmetic and copies ran while one was open for 0% of the time, Pallas kernels for 0%

profile of v1, /device:TPU:16, one launch (start us, length us, event | category | flops | bytes accessed | tf_op | source)
XLA Modules:
  0.0 56.1 jit_solution(5260465726216802590)
XLA Ops:
  0.6 0.0 copy-start
  0.6 1.1 %copy-done = f32[3,16,32,128]{3,2,1,0:T(8,128)S(1)} copy-done((f32[3,16,32,128]{3,2,1,0:T(8,128)S(1)}, f32[3,16,32,128]{3,2,1,0:T(8,128)}, u32[]{:S(2)}) %copy-start) | copy-done | bytes 786456
  1.8 0.9 %copy-done.1 = f32[16,32,128]{2,1,0:T(8,128)S(1)} copy-done((f32[16,32,128]{2,1,0:T(8,128)S(1)}, f32[16,32,128]{2,1,0:T(8,128)}, u32[]{:S(2)}) %copy-start.1) | copy-done | bytes 262168
  2.7 0.9 %copy-done.2 = f32[16,32,128]{2,1,0:T(8,128)S(1)} copy-done((f32[16,32,128]{2,1,0:T(8,128)S(1)}, f32[16,32,128]{2,1,0:T(8,128)}, u32[]{:S(2)}) %copy-start.2) | copy-done | bytes 262168
  3.7 0.4 edges.1
  4.1 0.1 collective-permute-start.2
  4.2 2.0 %collective-permute-start = (f32[5,2,32,128]{3,2,1,0:T(8,128)S(1)}, f32[5,2,32,128]{3,2,1,0:T(8,128)S(1)}, u32[]{:S(2)}, u32[]{:S(2)}) collective-permute-start(f32[5,2,32,128]{3,2,1,0:T(8,128)S(1)} %get-tuple-element.13), channel_id=1, source_target_pairs={{0,16},{16,32},{32,48},{48,64},{64,80},{80,96},{96,112},{112,128},... | collective-permute-start | bytes 491528 | tf_op jit(solution)/shard_map/ppermute | solution.py:215
  6.2 4.7 %collective-permute-start.1 = (f32[5,2,32,128]{3,2,1,0:T(8,128)S(1)}, f32[5,2,32,128]{3,2,1,0:T(8,128)S(1)}, u32[]{:S(2)}, u32[]{:S(2)}) collective-permute-start(f32[5,2,32,128]{3,2,1,0:T(8,128)S(1)} %get-tuple-element.14), channel_id=1, source_target_pairs={{0,240},{16,0},{32,16},{48,32},{64,48},{80,64},{96,80},{112,96},{1... | collective-permute-start | bytes 491528 | tf_op jit(solution)/shard_map/ppermute | solution.py:216
  10.9 2.2 %collective-permute-start.3 = (f32[5,2,16,128]{3,2,1,0:T(8,128)S(1)}, f32[5,2,16,128]{3,2,1,0:T(8,128)S(1)}, u32[]{:S(2)}, u32[]{:S(2)}) collective-permute-start(f32[5,2,16,128]{3,2,1,0:T(8,128)S(1)} %get-tuple-element.16), channel_id=1, source_target_pairs={{0,12},{4,0},{8,4},{12,8},{1,13},{5,1},{9,5},{13,9},{2,14},{6,2},{... | collective-permute-start | bytes 245768 | tf_op jit(solution)/shard_map/ppermute | solution.py:218
  13.1 2.8 %collective-permute-start.5 = (f32[5,32,128]{2,1,0:T(8,128)S(1)}, f32[5,32,128]{2,1,0:T(8,128)S(1)}, u32[]{:S(2)}, u32[]{:S(2)}) collective-permute-start(f32[5,32,128]{2,1,0:T(8,128)S(1)} %get-tuple-element.17), channel_id=1, source_target_pairs={{0,3},{1,0},{2,1},{3,2},{4,7},{5,4},{6,5},{7,6},{8,11},{9,8},{10,9... | collective-permute-start | bytes 245768 | tf_op jit(solution)/shard_map/ppermute | solution.py:220
  15.9 0.0 collective-permute-done.2.a_lo
  15.9 0.0 collective-permute-start.4
  15.9 0.0 collective-permute-done.3.a_hi
  15.9 2.0 %collective-permute-done.5.r_right = f32[5,32,128]{2,1,0:T(8,128)S(1)} collective-permute-done((f32[5,32,128]{2,1,0:T(8,128)S(1)}, f32[5,32,128]{2,1,0:T(8,128)S(1)}, u32[]{:S(2)}, u32[]{:S(2)}) %collective-permute-start.5) | collective-permute-done | bytes 81952 | tf_op jit(solution)/shard_map/ppermute | solution.py:220
  17.9 3.6 %collective-permute-done.4.r_left = f32[5,32,128]{2,1,0:T(8,128)S(1)} collective-permute-done((f32[5,32,128]{2,1,0:T(8,128)S(1)}, f32[5,32,128]{2,1,0:T(8,128)S(1)}, u32[]{:S(2)}, u32[]{:S(2)}) %collective-permute-start.4) | collective-permute-done | bytes 81952 | tf_op jit(solution)/shard_map/ppermute | solution.py:219
  21.5 0.0 collective-permute-done.s_lo
  21.5 0.0 collective-permute-done.1.s_hi
  21.6 0.0 copy-done.3
  21.6 5.7 %stencil.1 = (f32[16,32,128]{2,1,0:T(8,128)}, f32[3,16,32,128]{3,2,1,0:T(8,128)}, f32[16,32,128]{2,1,0:T(8,128)}, f32[32,16,128]{2,1,0:T(8,128)S(1)}) custom-call(f32[16,32,128]{2,1,0:T(8,128)S(1)} %copy-done.1, f32[3,16,32,128]{3,2,1,0:T(8,128)S(1)} %copy-done, f32[16,32,128]{2,1,0:T(8,128)S(1)} %copy-done.2, f32[16,32,128]{2,1,0:T(8,128)S(1)} %copy-done.3, ...), custom_call_target="tpu_custom_call" | custom-call | tf_op jit(solution)/shard_map/stencil/pallas_call | solution.py:221
  27.3 15.1 %all_to_all.10.spread = f32[16,2,16,128]{3,2,1,0:T(8,128)S(1)} all-to-all(f32[16,2,16,128]{3,2,1,0:T(8,128)S(1)} %bitcast.3), channel_id=1, replica_groups=mesh['sector'=16,'ax'=4,'rad'=4] {'sector'}, dimensions={0} | all-to-all | bytes 524288 | tf_op jit(solution)/shard_map/all_to_all | solution.py:246
  42.4 0.0 copy-done.4
  42.4 0.4 harmonics.1
  42.8 12.7 %all_to_all.11 = f32[16,2,8,128]{3,2,1,0:T(8,128)S(1)} all-to-all(f32[16,2,8,128]{3,2,1,0:T(8,128)S(1)} %harmonics.1), channel_id=1, replica_groups=mesh['sector'=16,'ax'=4,'rad'=4] {'sector'}, dimensions={0} | all-to-all | bytes 262144 | tf_op jit(solution)/shard_map/all_to_all | solution.py:255
  55.5 0.7 %gather.1 = f32[8,32,128]{2,1,0:T(8,128)} custom-call(f32[32,8,128]{2,1,0:T(8,128)S(1)} %bitcast.2), custom_call_target="tpu_custom_call" | custom-call | tf_op jit(solution)/shard_map/gather/pallas_call | solution.py:256
  (4 shorter events, 0.0 us)
Async XLA Ops:
  0.6 1.1 %copy-start = (f32[3,16,32,128]{3,2,1,0:T(8,128)S(1)}, f32[3,16,32,128]{3,2,1,0:T(8,128)}, u32[]{:S(2)}) copy-start(f32[3,16,32,128]{3,2,1,0:T(8,128)} %vel.3) | copy-start | bytes 2359300
  1.8 0.9 %copy-start.1 = (f32[16,32,128]{2,1,0:T(8,128)S(1)}, f32[16,32,128]{2,1,0:T(8,128)}, u32[]{:S(2)}) copy-start(f32[16,32,128]{2,1,0:T(8,128)} %rho.3) | copy-start | bytes 786436
  2.7 0.9 %copy-start.2 = (f32[16,32,128]{2,1,0:T(8,128)S(1)}, f32[16,32,128]{2,1,0:T(8,128)}, u32[]{:S(2)}) copy-start(f32[16,32,128]{2,1,0:T(8,128)} %temp.3) | copy-start | bytes 786436
  3.7 17.9 %copy-start.3 = (f32[16,32,128]{2,1,0:T(8,128)S(1)}, f32[16,32,128]{2,1,0:T(8,128)}, u32[]{:S(2)}) copy-start(f32[16,32,128]{2,1,0:T(8,128)} %heat.1) | copy-start | bytes 786436
  4.1 11.8 %collective-permute-start.2 = (f32[5,2,16,128]{3,2,1,0:T(8,128)S(1)}, f32[5,2,16,128]{3,2,1,0:T(8,128)S(1)}, u32[]{:S(2)}, u32[]{:S(2)}) collective-permute-start(f32[5,2,16,128]{3,2,1,0:T(8,128)S(1)} %get-tuple-element.15), channel_id=1, source_target_pairs={{0,4},{4,8},{8,12},{12,0},{1,5},{5,9},{9,13},{13,1},{2,6},{6,10},{... | collective-permute-start | bytes 245768 | tf_op jit(solution)/shard_map/ppermute | solution.py:217
  4.2 17.3 %collective-permute-start = (f32[5,2,32,128]{3,2,1,0:T(8,128)S(1)}, f32[5,2,32,128]{3,2,1,0:T(8,128)S(1)}, u32[]{:S(2)}, u32[]{:S(2)}) collective-permute-start(f32[5,2,32,128]{3,2,1,0:T(8,128)S(1)} %get-tuple-element.13), channel_id=1, source_target_pairs={{0,16},{16,32},{32,48},{48,64},{64,80},{80,96},{96,112},{112,128},... | collective-permute-start | bytes 491528 | tf_op jit(solution)/shard_map/ppermute | solution.py:215
  6.2 15.3 %collective-permute-start.1 = (f32[5,2,32,128]{3,2,1,0:T(8,128)S(1)}, f32[5,2,32,128]{3,2,1,0:T(8,128)S(1)}, u32[]{:S(2)}, u32[]{:S(2)}) collective-permute-start(f32[5,2,32,128]{3,2,1,0:T(8,128)S(1)} %get-tuple-element.14), channel_id=1, source_target_pairs={{0,240},{16,0},{32,16},{48,32},{64,48},{80,64},{96,80},{112,96},{1... | collective-permute-start | bytes 491528 | tf_op jit(solution)/shard_map/ppermute | solution.py:216
  10.9 5.0 %collective-permute-start.3 = (f32[5,2,16,128]{3,2,1,0:T(8,128)S(1)}, f32[5,2,16,128]{3,2,1,0:T(8,128)S(1)}, u32[]{:S(2)}, u32[]{:S(2)}) collective-permute-start(f32[5,2,16,128]{3,2,1,0:T(8,128)S(1)} %get-tuple-element.16), channel_id=1, source_target_pairs={{0,12},{4,0},{8,4},{12,8},{1,13},{5,1},{9,5},{13,9},{2,14},{6,2},{... | collective-permute-start | bytes 245768 | tf_op jit(solution)/shard_map/ppermute | solution.py:218
  13.1 4.8 %collective-permute-start.5 = (f32[5,32,128]{2,1,0:T(8,128)S(1)}, f32[5,32,128]{2,1,0:T(8,128)S(1)}, u32[]{:S(2)}, u32[]{:S(2)}) collective-permute-start(f32[5,32,128]{2,1,0:T(8,128)S(1)} %get-tuple-element.17), channel_id=1, source_target_pairs={{0,3},{1,0},{2,1},{3,2},{4,7},{5,4},{6,5},{7,6},{8,11},{9,8},{10,9... | collective-permute-start | bytes 245768 | tf_op jit(solution)/shard_map/ppermute | solution.py:220
  15.9 5.7 %collective-permute-start.4 = (f32[5,32,128]{2,1,0:T(8,128)S(1)}, f32[5,32,128]{2,1,0:T(8,128)S(1)}, u32[]{:S(2)}, u32[]{:S(2)}) collective-permute-start(f32[5,32,128]{2,1,0:T(8,128)S(1)} %get-tuple-element.17), channel_id=1, source_target_pairs={{0,1},{1,2},{2,3},{3,0},{4,5},{5,6},{6,7},{7,4},{8,9},{9,10},{10,1... | collective-permute-start | bytes 245768 | tf_op jit(solution)/shard_map/ppermute | solution.py:219
  27.3 15.1 %copy-start.4 = (f32[128,256]{1,0:T(8,128)S(1)}, f32[128,256]{1,0:T(8,128)}, u32[]{:S(2)}) copy-start(f32[128,256]{1,0:T(8,128)} %constant.2.clone.table) | copy-start | bytes 393220

commit v2 on v1

v2 whole, which is shorter than its diff:
```python
import math

import jax
import jax.numpy as jnp
import numpy as np
from jax import lax
from jax.experimental import pallas as pl
from jax.experimental.pallas import tpu as pltpu
from jax.sharding import PartitionSpec as P

HARM = 128
HEAT_RATIO = 1.4
STEP_DT = 0.1
VISCOSITY = 0.1
DIFFUSIVITY = 0.1
VMEM_LIMIT = 16 * 1024 * 1024


def basis_table(ntheta):
    half = HARM // 2
    rows = np.arange(HARM)
    orders = np.where(rows <= half, rows, rows - half)
    phase = orders[:, None] * np.arange(ntheta)[None, :] % ntheta
    angle = phase * (2.0 * math.pi / ntheta)
    values = np.where((rows > half)[:, None], np.sin(angle), np.cos(angle))
    return (values / math.sqrt(ntheta)).astype(np.float32)


def edge_rows(ref, f, first, count, stride):
    lead, rows, lanes = ref.shape[1:]
    return ref.at[f].reshape(lead * rows, lanes).at[pl.ds(first, count, stride=stride), :]


def edges_kernel(rho, vel, temp, s_lo, s_hi, a_lo, a_hi, r_pack, held, sems):
    nt, na, nr = rho.shape
    sources = [rho, vel.at[0], vel.at[1], vel.at[2], temp]
    copies = [
        pltpu.make_async_copy(src, held.at[f], sems.at[f]) for f, src in enumerate(sources)
    ]
    for copy in copies:
        copy.start()
    lane = lax.broadcasted_iota(jnp.int32, (na, nr), 1)
    for f, copy in enumerate(copies):
        copy.wait()
        s_lo[f] = held[f, 0:2]
        s_hi[f] = held[f, nt - 2 : nt]
        for side in range(2):
            a_lo[f, side] = edge_rows(held, f, side, nt, na)[...]
            a_hi[f, side] = edge_rows(held, f, na - 2 + side, nt, na)[...]
        shift = 4 * (f % 2)
        packed = r_pack[f // 2] if f % 2 else jnp.zeros((na, nr), jnp.float32)
        for t in range(nt):
            turn = (8 * t + shift) % nr
            x = held[f, t]
            turned = pltpu.roll(x, turn, 1) if turn else x
            near = (lane + 2 - turn) % nr < 4
            packed = jnp.where(near, turned, packed)
        r_pack[f // 2] = packed


def place():
    ax, rad = lax.axis_index("ax"), lax.axis_index("rad")
    nax, nrad = lax.axis_size("ax"), lax.axis_size("rad")
    keep = [
        jnp.where(c, 1.0, 0.0) for c in (ax > 0, ax < nax - 1, rad > 0, rad < nrad - 1)
    ]
    return keep, rad, nrad


def fill(pad, halos, r_halo, keep):
    s_lo, s_hi, a_lo, a_hi, r_left, r_right = halos
    nt, na, nr = pad.shape[1] - 4, pad.shape[2] - 16, pad.shape[3]
    rows = na + 16
    for f in range(5):
        pad[f, 0:2, 8 : 8 + na] = s_lo[f]
        pad[f, nt + 2 : nt + 4, 8 : 8 + na] = s_hi[f]
    for f in range(5):
        for side in range(2):
            edge_rows(pad, f, 2 * rows + 6 + side, nt, rows)[...] = a_lo[f, side] * keep[0]
            edge_rows(pad, f, 2 * rows + 8 + na + side, nt, rows)[...] = a_hi[f, side] * keep[1]
    join_packs(r_halo, r_left, r_right, keep)


def join_packs(r_halo, r_left, r_right, keep):
    mod4 = lax.broadcasted_iota(jnp.int32, r_left.shape[1:], 1) % 4
    for q in range(r_left.shape[0]):
        r_halo[q] = jnp.where(mod4 < 2, r_right[q] * keep[3], r_left[q] * keep[2])


def spacings(rad, nrad, nr):
    lane = lax.broadcasted_iota(jnp.int32, (8, nr), 1)
    radius = (rad * nr + lane).astype(jnp.float32)
    h = 0.5 + (radius + 0.5) / (nr * nrad)
    return 1.0 / (12.0 * h), VISCOSITY / (12.0 * h * h), lane


def d1(s):
    return 8.0 * (s[2] - s[1]) - (s[3] - s[0])


def lane_shifts(mid, halo, lane):
    nr = mid.shape[-1]
    return [
        pltpu.roll(jnp.where(lane >= nr - 2, halo, mid), 2, 1),
        pltpu.roll(jnp.where(lane == nr - 1, halo, mid), 1, 1),
        pltpu.roll(jnp.where(lane == 0, halo, mid), nr - 1, 1),
        pltpu.roll(jnp.where(lane < 2, halo, mid), nr - 2, 1),
    ]


def t_shifts(ref, t, lo):
    return [ref[t + 2 + d, lo : lo + 8] for d in (-2, -1, 1, 2)]


def a_shifts(ref, t, lo):
    return [ref[t + 2, lo + d : lo + d + 8] for d in (-2, -1, 1, 2)]


def transport(mid, st, sa, sr, w, gt):
    ring1 = (sa[1] + sa[2]) + (sr[1] + sr[2])
    ring2 = (sa[0] + sa[3]) + (sr[0] + sr[3])
    curve_t = 16.0 * (st[1] + st[2]) - 30.0 * mid - (st[0] + st[3])
    curve = 16.0 * ring1 - 60.0 * mid - ring2
    return gt * curve_t + (VISCOSITY / 12.0) * curve - (
        w[0] * d1(st) + w[1] * d1(sa) + w[2] * d1(sr)
    )


def inner_kernel(vel, temp, heat, base, pad):
    nt, na, nr = heat.shape
    rad, nrad = lax.axis_index("rad"), lax.axis_size("rad")
    zeros = jnp.zeros((2, na, nr), jnp.float32)
    for q, ref in enumerate((vel.at[0], vel.at[1], temp)):
        pad[q, 2 : nt + 2, 8 : 8 + na] = ref[...]
        pad[q, 0:2, 8 : 8 + na] = zeros
        pad[q, nt + 2 : nt + 4, 8 : 8 + na] = zeros
        for t in range(nt):
            pad[q, t + 2, 0:8] = zeros[0, 0:8]
            pad[q, t + 2, 8 + na : 16 + na] = zeros[0, 0:8]
    inv12h, gt, lane = spacings(rad, nrad, nr)
    inv12 = 1.0 / 12.0

    def step(t, carry):
        for j in range(na // 8):
            lo, out = 8 + j * 8, slice(j * 8, j * 8 + 8)
            u = [vel[c, t, out] for c in range(3)]
            w = [u[0] * inv12h, u[1] * inv12, u[2] * inv12]
            div = (
                d1(t_shifts(pad.at[0], t, lo)) * inv12h
                + (d1(a_shifts(pad.at[1], t, lo)) + d1(lane_shifts(u[2], 0.0, lane))) * inv12
            )
            mid = temp[t, out]
            rate = transport(
                mid,
                t_shifts(pad.at[2], t, lo),
                a_shifts(pad.at[2], t, lo),
                lane_shifts(mid, 0.0, lane),
                w,
                gt,
            )
            rate = rate - (HEAT_RATIO - 1.0) * (1.0 + mid) * div + heat[t, out]
            base[t, out] = mid + STEP_DT * rate
        return carry

    lax.fori_loop(0, nt, step, 0, unroll=2)


def low_parts(n, place):
    if place == 0:
        return n[0] - 8.0 * n[1], 16.0 * n[1] - n[0]
    return n[1], -n[1]


def high_parts(p, place):
    if place == 0:
        return 8.0 * p[0] - p[1], 16.0 * p[0] - p[1]
    return -p[0], -p[0]


def halo_share(mid, u, c, g, t_parts, u_parts):
    slope, curve = t_parts
    return STEP_DT * (
        g * curve - c * (u * slope + (HEAT_RATIO - 1.0) * (1.0 + mid) * u_parts[0])
    )


def pack_parts(x):
    nr = x.shape[-1]
    mod4 = lax.broadcasted_iota(jnp.int32, x.shape, 1) % 4
    up1, up2 = pltpu.roll(x, nr - 1, 1), pltpu.roll(x, nr - 2, 1)
    down1, down2 = pltpu.roll(x, 1, 1), pltpu.roll(x, 2, 1)
    above, inner, outer = mod4 >= 2, mod4 == 3, mod4 == 0
    slope = jnp.where(
        above,
        jnp.where(inner, 8.0 * up1, 0.0) - up2,
        down2 - jnp.where(outer, 8.0 * down1, 0.0),
    )
    curve = jnp.where(
        above,
        jnp.where(inner, 16.0 * up1, 0.0) - up2,
        jnp.where(outer, 16.0 * down1, 0.0) - down2,
    )
    return slope, curve


def temperature_kernel(
    vel, temp, base, s_lo, s_hi, a_lo, a_hi, r_left, r_right, cells, r_halo
):
    nt, na, nr = base.shape
    keep, rad, nrad = place()
    join_packs(r_halo, r_left, r_right, keep)
    inv12h, gt, lane = spacings(rad, nrad, nr)
    inv12, g = 1.0 / 12.0, VISCOSITY / 12.0
    turned = cells.reshape(na * nt, nr)
    edge = (lane < 2) | (lane >= nr - 2)
    u_slope, _ = pack_parts(r_halo[1])
    t_slope, t_curve = pack_parts(r_halo[2])
    for t in range(nt):
        even, odd = (nr - 8 * t) % nr, (2 * nr - 8 * t - 4) % nr
        ts = pltpu.roll(t_slope, even, 1) if even else t_slope
        tc = pltpu.roll(t_curve, even, 1) if even else t_curve
        us = pltpu.roll(u_slope, odd, 1) if odd else u_slope
        for j in range(na // 8):
            out = slice(j * 8, j * 8 + 8)
            mid = temp[t, out]
            share = halo_share(mid, vel[2, t, out], inv12, g, (ts[out], tc[out]), (us[out],))
            value = base[t, out] + jnp.where(edge, share, 0.0)
            parts = None
            if t < 2:
                parts = [low_parts((s_lo[f, 0, out], s_lo[f, 1, out]), t) for f in (4, 1)]
            elif t >= nt - 2:
                parts = [
                    high_parts((s_hi[f, 0, out], s_hi[f, 1, out]), nt - 1 - t) for f in (4, 1)
                ]
            if parts is not None:
                value = value + halo_share(mid, vel[0, t, out], inv12h, gt, *parts)
            turned[pl.ds(j * 8 * nt + t, 8, stride=nt), :] = value
    rows, speeds = temp.reshape(nt * na, nr), vel.at[1].reshape(nt * na, nr)
    for a in (0, 1, na - 2, na - 1):
        mid, u = rows[pl.ds(a, nt, stride=na), :], speeds[pl.ds(a, nt, stride=na), :]
        if a < 2:
            parts = [low_parts((a_lo[f, 0], a_lo[f, 1]), a) for f in (4, 2)]
            scale = keep[0]
        else:
            parts = [high_parts((a_hi[f, 0], a_hi[f, 1]), na - 1 - a) for f in (4, 2)]
            scale = keep[1]
        cells[a] = cells[a] + scale * halo_share(mid, u, inv12, g, *parts)


def flow_kernel(
    rho, vel, temp, cells, s_lo, s_hi, a_lo, a_hi, r_left, r_right,
    new_rho, new_vel, new_temp,
    full, flux_t, flux_a, flux_r, press, r_halo,
):
    nt, na, nr = new_rho.shape
    keep, rad, nrad = place()
    for f, ref in enumerate((rho, vel.at[0], vel.at[1], vel.at[2], temp)):
        full[f, 2 : nt + 2, 8 : 8 + na] = ref[...]
    halos = (s_lo, s_hi, a_lo, a_hi, r_left, r_right)
    fill(full, halos, r_halo, keep)

    def products(t, carry):
        mass = 1.0 + full[0, t]
        flux_t[t] = mass * full[1, t]
        press[t] = mass * (1.0 + full[4, t])
        return carry

    lax.fori_loop(0, nt + 4, products, 0)

    def products_in(t, carry):
        mass = 1.0 + full[0, t + 2]
        flux_a[t + 2] = mass * full[2, t + 2]
        flux_r[t] = mass[8 : 8 + na] * full[3, t + 2, 8 : 8 + na]
        return carry

    lax.fori_loop(0, nt, products_in, 0)
    inv12h, gt, lane = spacings(rad, nrad, nr)
    inv12 = 1.0 / 12.0
    turned = cells.reshape(na * nt, nr)

    def step(t, carry):
        even, odd = (nr - 8 * t) % nr, (2 * nr - 8 * t - 4) % nr
        hr, h0, h1, h2, ht = [
            pltpu.roll(r_halo[f // 2], odd if f % 2 else even, 1) for f in range(5)
        ]
        turned_halo = [h0, h1, h2, (1.0 + hr) * h2, (1.0 + hr) * (1.0 + ht)]
        for j in range(na // 8):
            lo, out = 8 + j * 8, slice(j * 8, j * 8 + 8)
            halo = [x[out] for x in turned_halo]
            r0 = full[0, t + 2, lo : lo + 8]
            u = [full[1 + c, t + 2, lo : lo + 8] for c in range(3)]
            w = [u[0] * inv12h, u[1] * inv12, u[2] * inv12]
            scale = 1.0 / (HEAT_RATIO * (1.0 + r0))
            grads = [
                d1(t_shifts(press, t, lo)) * inv12h,
                d1(a_shifts(press, t, lo)) * inv12,
                d1(lane_shifts(press[t + 2, lo : lo + 8], halo[4], lane)) * inv12,
            ]
            for c in range(3):
                ref = full.at[1 + c]
                rate = transport(
                    u[c],
                    t_shifts(ref, t, lo),
                    a_shifts(ref, t, lo),
                    lane_shifts(u[c], halo[c], lane),
                    w,
                    gt,
                )
                new_vel[c, t, out] = u[c] + STEP_DT * (rate - grads[c] * scale)
            loss = (
                d1(t_shifts(flux_t, t, lo)) * inv12h
                + (
                    d1(a_shifts(flux_a, t, lo))
                    + d1(lane_shifts(flux_r[t, out], halo[3], lane))
                )
                * inv12
            )
            new_rho[t, out] = r0 - STEP_DT * loss
            new_temp[t, out] = turned[pl.ds(j * 8 * nt + t, 8, stride=nt), :]
        return carry

    lax.fori_loop(0, nt, step, 0)


def harmonics_kernel(table, spread, out, held, sems):
    sectors, parts, nt, nr = spread.shape
    copies = []
    for p in range(parts):
        x = spread[:, p].reshape(sectors * nt, nr)
        y = jnp.dot(
            table[...], x, precision=lax.Precision.HIGHEST, preferred_element_type=jnp.float32
        )
        held[p] = y.reshape(sectors, HARM // sectors, nr)
        copies.append(pltpu.make_async_copy(held.at[p], out.at[:, p], sems.at[p]))
        copies[p].start()
    for copy in copies:
        copy.wait()


def gather_kernel(parts, out):
    cells, rows, nr = parts.shape
    flat = parts.reshape(cells * rows, nr)
    for k in range(rows):
        out[k] = flat[pl.ds(k, cells, stride=rows), :]


def per_device(table, mass_excess, speed_vector, thermal_excess, energy_release):
    nt, na, nr = mass_excess.shape
    f32 = jnp.float32
    params = pltpu.CompilerParams(vmem_limit_bytes=VMEM_LIMIT)
    sds = jax.ShapeDtypeStruct
    hbm = pl.BlockSpec(memory_space=pltpu.HBM)
    vmem = pl.BlockSpec(memory_space=pltpu.VMEM)
    padded = (nt + 4, na + 16, nr)
    s_lo, s_hi, a_lo, a_hi, r_pack = pl.pallas_call(
        edges_kernel,
        in_specs=[hbm] * 3,
        out_specs=[vmem] * 5,
        out_shape=(
            sds((5, 2, na, nr), f32),
            sds((5, 2, na, nr), f32),
            sds((5, 2, nt, nr), f32),
            sds((5, 2, nt, nr), f32),
            sds((3, na, nr), f32),
        ),
        scratch_shapes=[pltpu.VMEM((5, nt, na, nr), f32), pltpu.SemaphoreType.DMA((5,))],
        compiler_params=pltpu.CompilerParams(vmem_limit_bytes=54784 * 1024),
        name="edges",
    )(mass_excess, speed_vector, thermal_excess)

    def ring(axis, up):
        count = lax.axis_size(axis)
        return [(i, (i + (1 if up else -1)) % count) for i in range(count)]

    halos = (
        lax.ppermute(s_hi, "sector", ring("sector", True)),
        lax.ppermute(s_lo, "sector", ring("sector", False)),
        lax.ppermute(a_hi, "ax", ring("ax", True)),
        lax.ppermute(a_lo, "ax", ring("ax", False)),
        lax.ppermute(r_pack, "rad", ring("rad", True)),
        lax.ppermute(r_pack, "rad", ring("rad", False)),
    )
    (base,) = pl.pallas_call(
        inner_kernel,
        in_specs=[vmem] * 3,
        out_specs=[vmem],
        out_shape=(sds((nt, na, nr), f32),),
        scratch_shapes=[pltpu.VMEM((3, *padded), f32)],
        cost_estimate=pl.CostEstimate(
            flops=80 * nt * na * nr, bytes_accessed=24 * nt * na * nr, transcendentals=0
        ),
        compiler_params=params,
        name="inner",
    )(speed_vector, thermal_excess, energy_release)
    (cells,) = pl.pallas_call(
        temperature_kernel,
        in_specs=[vmem] * 9,
        out_specs=[vmem],
        out_shape=(sds((na, nt, nr), f32),),
        scratch_shapes=[pltpu.VMEM((3, na, nr), f32)],
        compiler_params=params,
        name="temperature",
    )(speed_vector, thermal_excess, base, *halos)
    sectors = lax.axis_size("sector")
    rows = HARM // sectors
    share = na // sectors
    spread = lax.all_to_all(
        cells.reshape(sectors, share, nt, nr), "sector", 0, 0, tiled=True
    )
    new_rho, new_vel, new_temp = pl.pallas_call(
        flow_kernel,
        in_specs=[vmem] * 10,
        out_shape=(
            sds((nt, na, nr), f32),
            sds((3, nt, na, nr), f32),
            sds((nt, na, nr), f32),
        ),
        scratch_shapes=[
            pltpu.VMEM((5, *padded), f32),
            pltpu.VMEM(padded, f32),
            pltpu.VMEM(padded, f32),
            pltpu.VMEM((nt, na, nr), f32),
            pltpu.VMEM(padded, f32),
            pltpu.VMEM((3, na, nr), f32),
        ],
        cost_estimate=pl.CostEstimate(
            flops=180 * nt * na * nr, bytes_accessed=44 * nt * na * nr, transcendentals=0
        ),
        compiler_params=params,
        name="flow",
    )(mass_excess, speed_vector, thermal_excess, cells, *halos)
    terms = pl.pallas_call(
        harmonics_kernel,
        in_specs=[vmem] * 2,
        out_specs=hbm,
        out_shape=sds((sectors, share, rows, nr), f32),
        scratch_shapes=[
            pltpu.VMEM((share, sectors, rows, nr), f32),
            pltpu.SemaphoreType.DMA((share,)),
        ],
        compiler_params=params,
        name="harmonics",
    )(table, spread)
    terms = lax.all_to_all(terms, "sector", 0, 0, tiled=True)
    coeffs = pl.pallas_call(
        gather_kernel,
        out_shape=sds((rows, na, nr), f32),
        compiler_params=params,
        name="gather",
    )(terms.reshape(na, rows, nr))
    return (new_rho, new_vel, new_temp, coeffs)


def solution(mesh):
    cell = P("sector", "ax", "rad")
    vector = P(None, "sector", "ax", "rad")

    def run(mass_excess, speed_vector, thermal_excess, energy_release):
        table = jnp.asarray(basis_table(mass_excess.shape[0]))
        return jax.shard_map(
            per_device,
            mesh=mesh,
            in_specs=(P(), cell, vector, cell, cell),
            out_specs=(cell, vector, cell, cell),
            check_vma=False,
        )(table, mass_excess, speed_vector, thermal_excess, energy_release)

    return run
```

time: 56.4 us -> 51.1 us (0.906)
  the two profiles are of different devices: /device:TPU:16 before, /device:TPU:2 now
where the time goes in v2:
time: 51.1 us; the launch traced here: 50.9 us
  starting transfers between devices  17.6 us (34%)
  blocking collectives  16.4 us (32%)
  Pallas kernels  11.1 us (22%)
  waiting for transfers between devices  4.99 us (10%)
  between operations  0.74 us (1%)
    all_to_all x1, blocking collectives, per_device(): lax.all_to_all(cells.reshape(sectors, share, nt, nr), 'sector', 0, 0, til...  16.4 us
    pallas_call x1, Pallas kernels, per_device(): pl.pallas_call(flow_kernel, in_specs=[vmem] * 10, out_shape=(sds((nt, na,...  5.32 us
    ppermute x1, starting transfers between devices, per_device(): lax.ppermute(s_lo, 'sector', ring('sector', False))  5.04 us
    all_to_all x1, starting transfers between devices, per_device(): terms = lax.all_to_all(terms, 'sector', 0, 0, tiled=True)  4.74 us
    all_to_all x1, waiting for transfers between devices, per_device(): terms = lax.all_to_all(terms, 'sector', 0, 0, tiled=True)  3.25 us
    ppermute x1, starting transfers between devices, per_device(): lax.ppermute(a_lo, 'ax', ring('ax', False))  3.25 us
    pallas_call x1, Pallas kernels, per_device(): pl.pallas_call(edges_kernel, in_specs=[hbm] * 3, out_specs=[vmem] * 5, ou...  2.37 us
    ppermute x1, starting transfers between devices, per_device(): lax.ppermute(s_hi, 'sector', ring('sector', True))  1.99 us
  transfers between devices with their start and end apart: 7, of which 2 were waited for; matrix products, arithmetic and copies ran while one was open for 0% of the time, Pallas kernels for 13%

profile of v2, /device:TPU:2, one launch (start us, length us, event | category | flops | bytes accessed | tf_op | source)
XLA Modules:
  0.0 50.9 jit_solution(18380461745381368545)
XLA Ops:
  0.7 2.4 %edges.1 = (f32[5,2,32,128]{3,2,1,0:T(8,128)S(1)}, f32[5,2,32,128]{3,2,1,0:T(8,128)}, f32[5,2,16,128]{3,2,1,0:T(8,128)S(1)}, f32[5,2,16,128]{3,2,1,0:T(8,128)S(1)}, f32[3,32,128]{2,1,0:T(8,128)S(1)}) custom-call(f32[16,32,128]{2,1,0:T(8,128)} %rho.3, f32[3,16,32,128]{3,2,1,0:T(8,128)} %vel.7, f32[16,32,128]{2,1,0:T(8,128)} %temp.7), custom_call_target="tpu_custom_call" | custom-call | tf_op jit(solution)/shard_map/edges/pallas_call | solution.py:355
  3.0 2.0 %collective-permute-start = (f32[5,2,32,128]{3,2,1,0:T(8,128)}, f32[5,2,32,128]{3,2,1,0:T(8,128)S(1)}, u32[]{:S(2)}, u32[]{:S(2)}) collective-permute-start(f32[5,2,32,128]{3,2,1,0:T(8,128)} %get-tuple-element.12), channel_id=1, source_target_pairs={{0,16},{16,32},{32,48},{48,64},{64,80},{80,96},{96,112},{112,128},... | collective-permute-start | bytes 491528 | tf_op jit(solution)/shard_map/ppermute | solution.py:376
  5.0 5.0 %collective-permute-start.1 = (f32[5,2,32,128]{3,2,1,0:T(8,128)S(1)}, f32[5,2,32,128]{3,2,1,0:T(8,128)S(1)}, u32[]{:S(2)}, u32[]{:S(2)}) collective-permute-start(f32[5,2,32,128]{3,2,1,0:T(8,128)S(1)} %get-tuple-element.13), channel_id=1, source_target_pairs={{0,240},{16,0},{32,16},{48,32},{64,48},{80,64},{96,80},{112,96},{1... | collective-permute-start | bytes 491528 | tf_op jit(solution)/shard_map/ppermute | solution.py:377
  10.1 1.5 %collective-permute-start.4 = (f32[3,32,128]{2,1,0:T(8,128)S(1)}, f32[3,32,128]{2,1,0:T(8,128)S(1)}, u32[]{:S(2)}, u32[]{:S(2)}) collective-permute-start(f32[3,32,128]{2,1,0:T(8,128)S(1)} %get-tuple-element.16), channel_id=1, source_target_pairs={{0,1},{1,2},{2,3},{3,0},{4,5},{5,6},{6,7},{7,4},{8,9},{9,10},{10,1... | collective-permute-start | bytes 147464 | tf_op jit(solution)/shard_map/ppermute | solution.py:380
  11.6 0.0 collective-permute-start.2
  11.6 3.2 %collective-permute-start.3 = (f32[5,2,16,128]{3,2,1,0:T(8,128)S(1)}, f32[5,2,16,128]{3,2,1,0:T(8,128)S(1)}, u32[]{:S(2)}, u32[]{:S(2)}) collective-permute-start(f32[5,2,16,128]{3,2,1,0:T(8,128)S(1)} %get-tuple-element.15), channel_id=1, source_target_pairs={{0,12},{4,0},{8,4},{12,8},{1,13},{5,1},{9,5},{13,9},{2,14},{6,2},{... | collective-permute-start | bytes 245768 | tf_op jit(solution)/shard_map/ppermute | solution.py:379
  14.8 0.0 collective-permute-done.4.r_left
  14.8 1.1 %collective-permute-start.5 = (f32[3,32,128]{2,1,0:T(8,128)S(1)}, f32[3,32,128]{2,1,0:T(8,128)S(1)}, u32[]{:S(2)}, u32[]{:S(2)}) collective-permute-start(f32[3,32,128]{2,1,0:T(8,128)S(1)} %get-tuple-element.16), channel_id=1, source_target_pairs={{0,3},{1,0},{2,1},{3,2},{4,7},{5,4},{6,5},{7,6},{8,11},{9,8},{10,9... | collective-permute-start | bytes 147464 | tf_op jit(solution)/shard_map/ppermute | solution.py:381
  15.9 0.0 copy-done
  15.9 1.3 %inner.1.base = f32[16,32,128]{2,1,0:T(8,128)S(1)} custom-call(f32[3,16,32,128]{3,2,1,0:T(8,128)S(1)} %copy-done, f32[16,32,128]{2,1,0:T(8,128)S(1)} %copy-done.1, f32[16,32,128]{2,1,0:T(8,128)S(1)} %copy-done.3), custom_call_target="tpu_custom_call" | custom-call | flops 5242880 | bytes 1572864 | tf_op jit(solution)/shard_map/inner/pallas_call | solution.py:383
  17.2 1.7 %collective-permute-done.5.r_right = f32[3,32,128]{2,1,0:T(8,128)S(1)} collective-permute-done((f32[3,32,128]{2,1,0:T(8,128)S(1)}, f32[3,32,128]{2,1,0:T(8,128)S(1)}, u32[]{:S(2)}, u32[]{:S(2)}) %collective-permute-start.5) | collective-permute-done | bytes 49184 | tf_op jit(solution)/shard_map/ppermute | solution.py:381
  18.9 0.0 collective-permute-done.2.a_lo
  18.9 0.0 collective-permute-done.3.a_hi
  18.9 0.0 collective-permute-done.s_lo
  18.9 0.0 collective-permute-done.1.s_hi
  18.9 0.4 temperature.1.cells
  19.4 0.0 copy-start.4
  19.4 16.4 %all_to_all.10.spread = f32[16,2,16,128]{3,2,1,0:T(8,128)S(1)} all-to-all(f32[16,2,16,128]{3,2,1,0:T(8,128)S(1)} %bitcast.2), channel_id=1, replica_groups=mesh['sector'=16,'ax'=4,'rad'=4] {'sector'}, dimensions={0} | all-to-all | bytes 524288 | tf_op jit(solution)/shard_map/all_to_all | solution.py:407
  35.8 1.0 %harmonics.1 = f32[16,2,8,128]{3,2,1,0:T(8,128)} custom-call(f32[128,256]{1,0:T(8,128)S(1)} %copy-done.4, f32[16,2,16,128]{3,2,1,0:T(8,128)S(1)} %all_to_all.10.spread), custom_call_target="tpu_custom_call" | custom-call | tf_op jit(solution)/shard_map/harmonics/pallas_call | solution.py:432
  36.8 0.0 copy-start.2
  36.8 4.7 %all-to-all-start.1 = ((f32[16,2,8,128]{3,2,1,0:T(8,128)}), f32[16,2,8,128]{3,2,1,0:T(8,128)S(1)}, u32[]{:S(2)}, u32[]{:S(2)}) async-start(f32[16,2,8,128]{3,2,1,0:T(8,128)} %harmonics.1), calls=%async_computation.1 | async-start | bytes 262144 | tf_op jit(solution)/shard_map/all_to_all | solution.py:444
  41.6 5.3 %flow.1 = (f32[16,32,128]{2,1,0:T(8,128)}, f32[3,16,32,128]{3,2,1,0:T(8,128)}, f32[16,32,128]{2,1,0:T(8,128)}) custom-call(f32[16,32,128]{2,1,0:T(8,128)S(1)} %copy-done.2, f32[3,16,32,128]{3,2,1,0:T(8,128)S(1)} %copy-done, f32[16,32,128]{2,1,0:T(8,128)S(1)} %copy-done.1, f32[32,16,128]{2,1,0:T(8,128)S(1)} %temperature.1.cells, ...), custom_call_target="tpu_custom_call" | custom-call | flops 11796480 | bytes 2883584 | tf_op jit(solution)/shard_map/flow/pallas_call | solution.py:410
  46.9 3.2 %all-to-all-done.1 = f32[16,2,8,128]{3,2,1,0:T(8,128)S(1)} async-done(((f32[16,2,8,128]{3,2,1,0:T(8,128)}), f32[16,2,8,128]{3,2,1,0:T(8,128)S(1)}, u32[]{:S(2)}, u32[]{:S(2)}) %all-to-all-start.1) | async-done | bytes 131104 | tf_op jit(solution)/shard_map/all_to_all | solution.py:444
  50.2 0.7 %gather.1 = f32[8,32,128]{2,1,0:T(8,128)} custom-call(f32[32,8,128]{2,1,0:T(8,128)S(1)} %bitcast.3), custom_call_target="tpu_custom_call" | custom-call | tf_op jit(solution)/shard_map/gather/pallas_call | solution.py:445
  (7 shorter events, 0.0 us)
Async XLA Ops:
  0.6 15.3 %copy-start = (f32[3,16,32,128]{3,2,1,0:T(8,128)S(1)}, f32[3,16,32,128]{3,2,1,0:T(8,128)}, u32[]{:S(2)}) copy-start(f32[3,16,32,128]{3,2,1,0:T(8,128)} %vel.7) | copy-start | bytes 2359300
  0.6 15.3 %copy-start.1 = (f32[16,32,128]{2,1,0:T(8,128)S(1)}, f32[16,32,128]{2,1,0:T(8,128)}, u32[]{:S(2)}) copy-start(f32[16,32,128]{2,1,0:T(8,128)} %temp.7) | copy-start | bytes 786436
  0.7 15.3 %copy-start.3 = (f32[16,32,128]{2,1,0:T(8,128)S(1)}, f32[16,32,128]{2,1,0:T(8,128)}, u32[]{:S(2)}) copy-start(f32[16,32,128]{2,1,0:T(8,128)} %heat.1) | copy-start | bytes 786436
  3.0 15.9 %collective-permute-start = (f32[5,2,32,128]{3,2,1,0:T(8,128)}, f32[5,2,32,128]{3,2,1,0:T(8,128)S(1)}, u32[]{:S(2)}, u32[]{:S(2)}) collective-permute-start(f32[5,2,32,128]{3,2,1,0:T(8,128)} %get-tuple-element.12), channel_id=1, source_target_pairs={{0,16},{16,32},{32,48},{48,64},{64,80},{80,96},{96,112},{112,128},... | collective-permute-start | bytes 491528 | tf_op jit(solution)/shard_map/ppermute | solution.py:376
  5.0 13.9 %collective-permute-start.1 = (f32[5,2,32,128]{3,2,1,0:T(8,128)S(1)}, f32[5,2,32,128]{3,2,1,0:T(8,128)S(1)}, u32[]{:S(2)}, u32[]{:S(2)}) collective-permute-start(f32[5,2,32,128]{3,2,1,0:T(8,128)S(1)} %get-tuple-element.13), channel_id=1, source_target_pairs={{0,240},{16,0},{32,16},{48,32},{64,48},{80,64},{96,80},{112,96},{1... | collective-permute-start | bytes 491528 | tf_op jit(solution)/shard_map/ppermute | solution.py:377
  10.1 4.7 %collective-permute-start.4 = (f32[3,32,128]{2,1,0:T(8,128)S(1)}, f32[3,32,128]{2,1,0:T(8,128)S(1)}, u32[]{:S(2)}, u32[]{:S(2)}) collective-permute-start(f32[3,32,128]{2,1,0:T(8,128)S(1)} %get-tuple-element.16), channel_id=1, source_target_pairs={{0,1},{1,2},{2,3},{3,0},{4,5},{5,6},{6,7},{7,4},{8,9},{9,10},{10,1... | collective-permute-start | bytes 147464 | tf_op jit(solution)/shard_map/ppermute | solution.py:380
  11.6 7.3 %collective-permute-start.2 = (f32[5,2,16,128]{3,2,1,0:T(8,128)S(1)}, f32[5,2,16,128]{3,2,1,0:T(8,128)S(1)}, u32[]{:S(2)}, u32[]{:S(2)}) collective-permute-start(f32[5,2,16,128]{3,2,1,0:T(8,128)S(1)} %get-tuple-element.14), channel_id=1, source_target_pairs={{0,4},{4,8},{8,12},{12,0},{1,5},{5,9},{9,13},{13,1},{2,6},{6,10},{... | collective-permute-start | bytes 245768 | tf_op jit(solution)/shard_map/ppermute | solution.py:378
  11.6 7.3 %collective-permute-start.3 = (f32[5,2,16,128]{3,2,1,0:T(8,128)S(1)}, f32[5,2,16,128]{3,2,1,0:T(8,128)S(1)}, u32[]{:S(2)}, u32[]{:S(2)}) collective-permute-start(f32[5,2,16,128]{3,2,1,0:T(8,128)S(1)} %get-tuple-element.15), channel_id=1, source_target_pairs={{0,12},{4,0},{8,4},{12,8},{1,13},{5,1},{9,5},{13,9},{2,14},{6,2},{... | collective-permute-start | bytes 245768 | tf_op jit(solution)/shard_map/ppermute | solution.py:379
  14.8 4.1 %collective-permute-start.5 = (f32[3,32,128]{2,1,0:T(8,128)S(1)}, f32[3,32,128]{2,1,0:T(8,128)S(1)}, u32[]{:S(2)}, u32[]{:S(2)}) collective-permute-start(f32[3,32,128]{2,1,0:T(8,128)S(1)} %get-tuple-element.16), channel_id=1, source_target_pairs={{0,3},{1,0},{2,1},{3,2},{4,7},{5,4},{6,5},{7,6},{8,11},{9,8},{10,9... | collective-permute-start | bytes 147464 | tf_op jit(solution)/shard_map/ppermute | solution.py:381
  19.4 16.4 %copy-start.4 = (f32[128,256]{1,0:T(8,128)S(1)}, f32[128,256]{1,0:T(8,128)}, u32[]{:S(2)}) copy-start(f32[128,256]{1,0:T(8,128)} %constant.2.clone.table) | copy-start | bytes 393220
  36.8 4.8 %copy-start.2 = (f32[16,32,128]{2,1,0:T(8,128)S(1)}, f32[16,32,128]{2,1,0:T(8,128)}, u32[]{:S(2)}) copy-start(f32[16,32,128]{2,1,0:T(8,128)} %rho.3) | copy-start | bytes 786436
  36.8 13.3 %all-to-all-start.1 = ((f32[16,2,8,128]{3,2,1,0:T(8,128)}), f32[16,2,8,128]{3,2,1,0:T(8,128)S(1)}, u32[]{:S(2)}, u32[]{:S(2)}) async-start(f32[16,2,8,128]{3,2,1,0:T(8,128)} %harmonics.1), calls=%async_computation.1 | async-start | bytes 262144 | tf_op jit(solution)/shard_map/all_to_all | solution.py:444

commit v3 on v2

--- a/solution.py
+++ b/solution.py
@@ -14,6 +14,7 @@
 VISCOSITY = 0.1
 DIFFUSIVITY = 0.1
 VMEM_LIMIT = 16 * 1024 * 1024
+PACK_PLANES = 6
 
 
 def basis_table(ntheta):
@@ -31,27 +32,36 @@
     return ref.at[f].reshape(lead * rows, lanes).at[pl.ds(first, count, stride=stride), :]
 
 
-def edges_kernel(rho, vel, temp, s_lo, s_hi, a_lo, a_hi, r_pack, held, sems):
+def sector_edges_kernel(rho, vel, temp, s_lo, s_hi, sems):
+    nt = rho.shape[0]
+    copies = []
+    for f, src in enumerate((rho, vel.at[0], vel.at[1], vel.at[2], temp)):
+        copies.append(pltpu.make_async_copy(src.at[0:2], s_lo.at[f], sems.at[2 * f]))
+        copies.append(
+            pltpu.make_async_copy(src.at[nt - 2 : nt], s_hi.at[f], sems.at[2 * f + 1])
+        )
+    for copy in copies:
+        copy.start()
+    for copy in copies:
+        copy.wait()
+
+
+def tile_edges_kernel(after, rho, vel, temp, a_lo, a_hi, r_pack):
+    del after
     nt, na, nr = rho.shape
     sources = [rho, vel.at[0], vel.at[1], vel.at[2], temp]
-    copies = [
-        pltpu.make_async_copy(src, held.at[f], sems.at[f]) for f, src in enumerate(sources)
-    ]
-    for copy in copies:
-        copy.start()
+    r_pack[3:] = jnp.zeros((r_pack.shape[0] - 3, na, nr), jnp.float32)
     lane = lax.broadcasted_iota(jnp.int32, (na, nr), 1)
-    for f, copy in enumerate(copies):
-        copy.wait()
-        s_lo[f] = held[f, 0:2]
-        s_hi[f] = held[f, nt - 2 : nt]
+    for f, held in enumerate(sources):
+        flat = held.reshape(nt * na, nr)
         for side in range(2):
-            a_lo[f, side] = edge_rows(held, f, side, nt, na)[...]
-            a_hi[f, side] = edge_rows(held, f, na - 2 + side, nt, na)[...]
+            a_lo[f, side] = flat[pl.ds(side, nt, stride=na), :]
+            a_hi[f, side] = flat[pl.ds(na - 2 + side, nt, stride=na), :]
         shift = 4 * (f % 2)
         packed = r_pack[f // 2] if f % 2 else jnp.zeros((na, nr), jnp.float32)
         for t in range(nt):
             turn = (8 * t + shift) % nr
-            x = held[f, t]
+            x = held[t]
             turned = pltpu.roll(x, turn, 1) if turn else x
             near = (lane + 2 - turn) % nr < 4
             packed = jnp.where(near, turned, packed)
@@ -83,7 +93,7 @@
 
 def join_packs(r_halo, r_left, r_right, keep):
     mod4 = lax.broadcasted_iota(jnp.int32, r_left.shape[1:], 1) % 4
-    for q in range(r_left.shape[0]):
+    for q in range(3):
         r_halo[q] = jnp.where(mod4 < 2, r_right[q] * keep[3], r_left[q] * keep[2])
 
 
@@ -352,21 +362,27 @@
     hbm = pl.BlockSpec(memory_space=pltpu.HBM)
     vmem = pl.BlockSpec(memory_space=pltpu.VMEM)
     padded = (nt + 4, na + 16, nr)
-    s_lo, s_hi, a_lo, a_hi, r_pack = pl.pallas_call(
-        edges_kernel,
+    s_lo, s_hi = pl.pallas_call(
+        sector_edges_kernel,
         in_specs=[hbm] * 3,
-        out_specs=[vmem] * 5,
+        out_specs=[vmem] * 2,
+        out_shape=(sds((5, 2, na, nr), f32), sds((5, 2, na, nr), f32)),
+        scratch_shapes=[pltpu.SemaphoreType.DMA((10,))],
+        compiler_params=pltpu.CompilerParams(vmem_limit_bytes=54912 * 1024),
+        name="sector_edges",
+    )(mass_excess, speed_vector, thermal_excess)
+    a_lo, a_hi, r_pack = pl.pallas_call(
+        tile_edges_kernel,
+        in_specs=[vmem] * 4,
+        out_specs=[vmem] * 3,
         out_shape=(
-            sds((5, 2, na, nr), f32),
-            sds((5, 2, na, nr), f32),
             sds((5, 2, nt, nr), f32),
             sds((5, 2, nt, nr), f32),
-            sds((3, na, nr), f32),
+            sds((PACK_PLANES, na, nr), f32),
         ),
-        scratch_shapes=[pltpu.VMEM((5, nt, na, nr), f32), pltpu.SemaphoreType.DMA((5,))],
-        compiler_params=pltpu.CompilerParams(vmem_limit_bytes=54784 * 1024),
-        name="edges",
-    )(mass_excess, speed_vector, thermal_excess)
+        compiler_params=params,
+        name="tile_edges",
+    )(s_lo, mass_excess, speed_vector, thermal_excess)
 
     def ring(axis, up):
         count = lax.axis_size(axis)

time: 51.1 us -> 49.2 us (0.963)
  blocking collectives: 16.4 us -> 14.3 us
  Pallas kernels: 11.1 us -> 10.2 us
    all_to_all x1, blocking collectives: 16.4 us -> 14.3 us  [per_device(): lax.all_to_all(cells.reshape(sectors, share, nt, nr), 'sector', 0, 0, til...]
    ppermute x1, waiting for transfers between devices: 0.01 us -> 2.02 us  [per_device(): lax.ppermute(a_lo, 'ax', ring('ax', False))]
    ppermute x1, starting transfers between devices: 1.99 us -> 0.01 us  [per_device(): lax.ppermute(s_hi, 'sector', ring('sector', True))]
    ppermute x1, starting transfers between devices: 5.04 us -> 6.94 us  [per_device(): lax.ppermute(s_lo, 'sector', ring('sector', False))]
    ppermute x1, waiting for transfers between devices: 1.73 us -> 0.01 us  [per_device(): lax.ppermute(r_pack, 'rad', ring('rad', False))]
    pallas_call x1 -> x2, Pallas kernels: 2.37 us -> 1.52 us  [the longest x1 1.09 us: per_device(): pl.pallas_call(sector_edges_kernel, in_specs=[hbm] * 3, out_specs=[vmem]...]
    all_to_all x1, starting transfers between devices: 4.74 us -> 5.46 us  [per_device(): terms = lax.all_to_all(terms, 'sector', 0, 0, tiled=True)]
    ppermute x1, starting transfers between devices: 1.09 us -> 0.53 us  [per_device(): lax.ppermute(r_pack, 'rad', ring('rad', False))]
  transfers between devices with their start and end apart: 7 -> 7, of which waited for: 2 -> 2; matrix products, arithmetic and copies ran while one was open for 0% -> 0% of each run, Pallas kernels for 13% -> 14%
where the time goes in v3:
time: 49.2 us; the launch traced here: 48.5 us
  starting transfers between devices  17.4 us (35%)
  blocking collectives  14.3 us (29%)
  Pallas kernels  10.2 us (21%)
  waiting for transfers between devices  5.46 us (11%)
  between operations  0.74 us (2%)
    all_to_all x1, blocking collectives, per_device(): lax.all_to_all(cells.reshape(sectors, share, nt, nr), 'sector', 0, 0, til...  14.3 us
    ppermute x1, starting transfers between devices, per_device(): lax.ppermute(s_lo, 'sector', ring('sector', False))  6.94 us
    all_to_all x1, starting transfers between devices, per_device(): terms = lax.all_to_all(terms, 'sector', 0, 0, tiled=True)  5.46 us
    pallas_call x1, Pallas kernels, per_device(): pl.pallas_call(flow_kernel, in_specs=[vmem] * 10, out_shape=(sds((nt, na,...  5.32 us
    all_to_all x1, waiting for transfers between devices, per_device(): terms = lax.all_to_all(terms, 'sector', 0, 0, tiled=True)  3.43 us
    ppermute x1, starting transfers between devices, per_device(): lax.ppermute(a_lo, 'ax', ring('ax', False))  2.93 us
    ppermute x1, waiting for transfers between devices, per_device(): lax.ppermute(a_lo, 'ax', ring('ax', False))  2.02 us
    ppermute x1, starting transfers between devices, per_device(): lax.ppermute(r_pack, 'rad', ring('rad', True))  1.49 us
  transfers between devices with their start and end apart: 7, of which 2 were waited for; matrix products, arithmetic and copies ran while one was open for 0% of the time, Pallas kernels for 14%

profile of v3, /device:TPU:2, one launch (start us, length us, event | category | flops | bytes accessed | tf_op | source)
XLA Modules:
  0.0 48.5 jit_solution(12664749798808043104)
XLA Ops:
  0.7 1.1 %sector_edges.1 = (f32[5,2,32,128]{3,2,1,0:T(8,128)S(1)}, f32[5,2,32,128]{3,2,1,0:T(8,128)S(1)}) custom-call(f32[16,32,128]{2,1,0:T(8,128)} %rho.5, f32[3,16,32,128]{3,2,1,0:T(8,128)} %vel.9, f32[16,32,128]{2,1,0:T(8,128)} %temp.9), custom_call_target="tpu_custom_call" | custom-call | tf_op jit(solution)/shard_map/sector_edges/pallas_call | solution.py:365
  1.8 0.2 copy-done
  2.0 0.0 copy-done.1
  2.1 0.4 tile_edges.1
  2.5 0.1 collective-permute-start.2
  2.6 6.9 %collective-permute-start.1 = (f32[5,2,32,128]{3,2,1,0:T(8,128)S(1)}, f32[5,2,32,128]{3,2,1,0:T(8,128)S(1)}, u32[]{:S(2)}, u32[]{:S(2)}) collective-permute-start(f32[5,2,32,128]{3,2,1,0:T(8,128)S(1)} %get-tuple-element.13.after), channel_id=1, source_target_pairs={{0,240},{16,0},{32,16},{48,32},{64,48},{80,64},{96,80},{112,96},{1... | collective-permute-start | bytes 491528 | tf_op jit(solution)/shard_map/ppermute | solution.py:393
  9.5 0.0 collective-permute-start
  9.5 1.5 %collective-permute-start.4 = (f32[6,32,128]{2,1,0:T(8,128)S(1)}, f32[6,32,128]{2,1,0:T(8,128)S(1)}, u32[]{:S(2)}, u32[]{:S(2)}) collective-permute-start(f32[6,32,128]{2,1,0:T(8,128)S(1)} %get-tuple-element.16), channel_id=1, source_target_pairs={{0,1},{1,2},{2,3},{3,0},{4,5},{5,6},{6,7},{7,4},{8,9},{9,10},{10,1... | collective-permute-start | bytes 294920 | tf_op jit(solution)/shard_map/ppermute | solution.py:396
  11.0 0.5 %collective-permute-start.5 = (f32[6,32,128]{2,1,0:T(8,128)S(1)}, f32[6,32,128]{2,1,0:T(8,128)S(1)}, u32[]{:S(2)}, u32[]{:S(2)}) collective-permute-start(f32[6,32,128]{2,1,0:T(8,128)S(1)} %get-tuple-element.16), channel_id=1, source_target_pairs={{0,3},{1,0},{2,1},{3,2},{4,7},{5,4},{6,5},{7,6},{8,11},{9,8},{10,9... | collective-permute-start | bytes 294920 | tf_op jit(solution)/shard_map/ppermute | solution.py:397
  11.6 0.0 collective-permute-done.2.a_lo
  11.6 2.9 %collective-permute-start.3 = (f32[5,2,16,128]{3,2,1,0:T(8,128)S(1)}, f32[5,2,16,128]{3,2,1,0:T(8,128)S(1)}, u32[]{:S(2)}, u32[]{:S(2)}) collective-permute-start(f32[5,2,16,128]{3,2,1,0:T(8,128)S(1)} %get-tuple-element.15), channel_id=1, source_target_pairs={{0,12},{4,0},{8,4},{12,8},{1,13},{5,1},{9,5},{13,9},{2,14},{6,2},{... | collective-permute-start | bytes 245768 | tf_op jit(solution)/shard_map/ppermute | solution.py:395
  14.5 1.3 %inner.1.base = f32[16,32,128]{2,1,0:T(8,128)S(1)} custom-call(f32[3,16,32,128]{3,2,1,0:T(8,128)S(1)} %copy-done, f32[16,32,128]{2,1,0:T(8,128)S(1)} %copy-done.1, f32[16,32,128]{2,1,0:T(8,128)S(1)} %copy-done.3), custom_call_target="tpu_custom_call" | custom-call | flops 5242880 | bytes 1572864 | tf_op jit(solution)/shard_map/inner/pallas_call | solution.py:399
  15.8 2.0 %collective-permute-done.3.a_hi = f32[5,2,16,128]{3,2,1,0:T(8,128)S(1)} collective-permute-done((f32[5,2,16,128]{3,2,1,0:T(8,128)S(1)}, f32[5,2,16,128]{3,2,1,0:T(8,128)S(1)}, u32[]{:S(2)}, u32[]{:S(2)}) %collective-permute-start.3) | collective-permute-done | bytes 81952 | tf_op jit(solution)/shard_map/ppermute | solution.py:395
  17.8 0.0 collective-permute-done.4.r_left
  17.8 0.0 collective-permute-done.5.r_right
  17.8 0.0 collective-permute-done.s_lo
  17.8 0.4 temperature.1.cells
  18.2 0.0 copy-start.4
  18.2 14.3 %all_to_all.10.spread = f32[16,2,16,128]{3,2,1,0:T(8,128)S(1)} all-to-all(f32[16,2,16,128]{3,2,1,0:T(8,128)S(1)} %bitcast.2), channel_id=1, replica_groups=mesh['sector'=16,'ax'=4,'rad'=4] {'sector'}, dimensions={0} | all-to-all | bytes 524288 | tf_op jit(solution)/shard_map/all_to_all | solution.py:423
  32.6 1.0 %harmonics.1 = f32[16,2,8,128]{3,2,1,0:T(8,128)} custom-call(f32[128,256]{1,0:T(8,128)S(1)} %copy-done.4, f32[16,2,16,128]{3,2,1,0:T(8,128)S(1)} %all_to_all.10.spread), custom_call_target="tpu_custom_call" | custom-call | tf_op jit(solution)/shard_map/harmonics/pallas_call | solution.py:448
  33.6 5.5 %all-to-all-start.1 = ((f32[16,2,8,128]{3,2,1,0:T(8,128)}), f32[16,2,8,128]{3,2,1,0:T(8,128)S(1)}, u32[]{:S(2)}, u32[]{:S(2)}) async-start(f32[16,2,8,128]{3,2,1,0:T(8,128)} %harmonics.1), calls=%async_computation.1 | async-start | bytes 262144 | tf_op jit(solution)/shard_map/all_to_all | solution.py:460
  39.1 5.3 %flow.1 = (f32[16,32,128]{2,1,0:T(8,128)}, f32[3,16,32,128]{3,2,1,0:T(8,128)}, f32[16,32,128]{2,1,0:T(8,128)}) custom-call(f32[16,32,128]{2,1,0:T(8,128)S(1)} %copy-done.2, f32[3,16,32,128]{3,2,1,0:T(8,128)S(1)} %copy-done, f32[16,32,128]{2,1,0:T(8,128)S(1)} %copy-done.1, f32[32,16,128]{2,1,0:T(8,128)S(1)} %temperature.1.cells, ...), custom_call_target="tpu_custom_call" | custom-call | flops 11796480 | bytes 2883584 | tf_op jit(solution)/shard_map/flow/pallas_call | solution.py:426
  44.4 3.4 %all-to-all-done.1 = f32[16,2,8,128]{3,2,1,0:T(8,128)S(1)} async-done(((f32[16,2,8,128]{3,2,1,0:T(8,128)}), f32[16,2,8,128]{3,2,1,0:T(8,128)S(1)}, u32[]{:S(2)}, u32[]{:S(2)}) %all-to-all-start.1) | async-done | bytes 131104 | tf_op jit(solution)/shard_map/all_to_all | solution.py:460
  47.8 0.7 %gather.1 = f32[8,32,128]{2,1,0:T(8,128)} custom-call(f32[32,8,128]{2,1,0:T(8,128)S(1)} %bitcast.3), custom_call_target="tpu_custom_call" | custom-call | tf_op jit(solution)/shard_map/gather/pallas_call | solution.py:461
  (8 shorter events, 0.0 us)
Async XLA Ops:
  0.6 1.1 %copy-start.2 = (f32[16,32,128]{2,1,0:T(8,128)S(1)}, f32[16,32,128]{2,1,0:T(8,128)}, u32[]{:S(2)}) copy-start(f32[16,32,128]{2,1,0:T(8,128)} %rho.5) | copy-start | bytes 786436
  0.6 1.4 %copy-start = (f32[3,16,32,128]{3,2,1,0:T(8,128)S(1)}, f32[3,16,32,128]{3,2,1,0:T(8,128)}, u32[]{:S(2)}) copy-start(f32[3,16,32,128]{3,2,1,0:T(8,128)} %vel.9) | copy-start | bytes 2359300
  0.7 1.4 %copy-start.1 = (f32[16,32,128]{2,1,0:T(8,128)S(1)}, f32[16,32,128]{2,1,0:T(8,128)}, u32[]{:S(2)}) copy-start(f32[16,32,128]{2,1,0:T(8,128)} %temp.9) | copy-start | bytes 786436
  2.1 12.4 %copy-start.3 = (f32[16,32,128]{2,1,0:T(8,128)S(1)}, f32[16,32,128]{2,1,0:T(8,128)}, u32[]{:S(2)}) copy-start(f32[16,32,128]{2,1,0:T(8,128)} %heat.1) | copy-start | bytes 786436
  2.5 9.1 %collective-permute-start.2 = (f32[5,2,16,128]{3,2,1,0:T(8,128)S(1)}, f32[5,2,16,128]{3,2,1,0:T(8,128)S(1)}, u32[]{:S(2)}, u32[]{:S(2)}) collective-permute-start(f32[5,2,16,128]{3,2,1,0:T(8,128)S(1)} %get-tuple-element.14), channel_id=1, source_target_pairs={{0,4},{4,8},{8,12},{12,0},{1,5},{5,9},{9,13},{13,1},{2,6},{6,10},{... | collective-permute-start | bytes 245768 | tf_op jit(solution)/shard_map/ppermute | solution.py:394
  2.6 15.2 %collective-permute-start.1 = (f32[5,2,32,128]{3,2,1,0:T(8,128)S(1)}, f32[5,2,32,128]{3,2,1,0:T(8,128)S(1)}, u32[]{:S(2)}, u32[]{:S(2)}) collective-permute-start(f32[5,2,32,128]{3,2,1,0:T(8,128)S(1)} %get-tuple-element.13.after), channel_id=1, source_target_pairs={{0,240},{16,0},{32,16},{48,32},{64,48},{80,64},{96,80},{112,96},{1... | collective-permute-start | bytes 491528 | tf_op jit(solution)/shard_map/ppermute | solution.py:393
  9.5 8.3 %collective-permute-start = (f32[5,2,32,128]{3,2,1,0:T(8,128)S(1)}, f32[5,2,32,128]{3,2,1,0:T(8,128)S(1)}, u32[]{:S(2)}, u32[]{:S(2)}) collective-permute-start(f32[5,2,32,128]{3,2,1,0:T(8,128)S(1)} %get-tuple-element.12), channel_id=1, source_target_pairs={{0,16},{16,32},{32,48},{48,64},{64,80},{80,96},{96,112},{112,128},... | collective-permute-start | bytes 491528 | tf_op jit(solution)/shard_map/ppermute | solution.py:392
  9.5 8.2 %collective-permute-start.4 = (f32[6,32,128]{2,1,0:T(8,128)S(1)}, f32[6,32,128]{2,1,0:T(8,128)S(1)}, u32[]{:S(2)}, u32[]{:S(2)}) collective-permute-start(f32[6,32,128]{2,1,0:T(8,128)S(1)} %get-tuple-element.16), channel_id=1, source_target_pairs={{0,1},{1,2},{2,3},{3,0},{4,5},{5,6},{6,7},{7,4},{8,9},{9,10},{10,1... | collective-permute-start | bytes 294920 | tf_op jit(solution)/shard_map/ppermute | solution.py:396
  11.0 6.8 %collective-permute-start.5 = (f32[6,32,128]{2,1,0:T(8,128)S(1)}, f32[6,32,128]{2,1,0:T(8,128)S(1)}, u32[]{:S(2)}, u32[]{:S(2)}) collective-permute-start(f32[6,32,128]{2,1,0:T(8,128)S(1)} %get-tuple-element.16), channel_id=1, source_target_pairs={{0,3},{1,0},{2,1},{3,2},{4,7},{5,4},{6,5},{7,6},{8,11},{9,8},{10,9... | collective-permute-start | bytes 294920 | tf_op jit(solution)/shard_map/ppermute | solution.py:397
  11.6 6.2 %collective-permute-start.3 = (f32[5,2,16,128]{3,2,1,0:T(8,128)S(1)}, f32[5,2,16,128]{3,2,1,0:T(8,128)S(1)}, u32[]{:S(2)}, u32[]{:S(2)}) collective-permute-start(f32[5,2,16,128]{3,2,1,0:T(8,128)S(1)} %get-tuple-element.15), channel_id=1, source_target_pairs={{0,12},{4,0},{8,4},{12,8},{1,13},{5,1},{9,5},{13,9},{2,14},{6,2},{... | collective-permute-start | bytes 245768 | tf_op jit(solution)/shard_map/ppermute | solution.py:395
  18.2 14.3 %copy-start.4 = (f32[128,256]{1,0:T(8,128)S(1)}, f32[128,256]{1,0:T(8,128)}, u32[]{:S(2)}) copy-start(f32[128,256]{1,0:T(8,128)} %constant.2.clone.table) | copy-start | bytes 393220
  33.6 14.2 %all-to-all-start.1 = ((f32[16,2,8,128]{3,2,1,0:T(8,128)}), f32[16,2,8,128]{3,2,1,0:T(8,128)S(1)}, u32[]{:S(2)}, u32[]{:S(2)}) async-start(f32[16,2,8,128]{3,2,1,0:T(8,128)} %harmonics.1), calls=%async_computation.1 | async-start | bytes 262144 | tf_op jit(solution)/shard_map/all_to_all | solution.py:460

commit v4 on v3

--- a/solution.py
+++ b/solution.py
@@ -32,39 +32,48 @@
     return ref.at[f].reshape(lead * rows, lanes).at[pl.ds(first, count, stride=stride), :]
 
 
-def sector_edges_kernel(rho, vel, temp, s_lo, s_hi, sems):
+def is_even(axis):
+    return lax.axis_index(axis) % 2 == 0
+
+
+def sector_edges_kernel(rho, vel, temp, far, near, sems):
     nt = rho.shape[0]
+    even = is_even("sector")
+    near_at, far_at = jnp.where(even, nt - 2, 0), jnp.where(even, 0, nt - 2)
     copies = []
     for f, src in enumerate((rho, vel.at[0], vel.at[1], vel.at[2], temp)):
-        copies.append(pltpu.make_async_copy(src.at[0:2], s_lo.at[f], sems.at[2 * f]))
-        copies.append(
-            pltpu.make_async_copy(src.at[nt - 2 : nt], s_hi.at[f], sems.at[2 * f + 1])
-        )
+        for out, at in ((far, far_at), (near, near_at)):
+            copies.append(
+                pltpu.make_async_copy(src.at[pl.ds(at, 2)], out.at[f], sems.at[len(copies)])
+            )
     for copy in copies:
         copy.start()
     for copy in copies:
         copy.wait()
 
 
-def tile_edges_kernel(after, rho, vel, temp, a_lo, a_hi, r_pack):
+def tile_edges_kernel(after, rho, vel, temp, near, far, r_pack):
     del after
     nt, na, nr = rho.shape
     sources = [rho, vel.at[0], vel.at[1], vel.at[2], temp]
+    even = is_even("ax")
     r_pack[3:] = jnp.zeros((r_pack.shape[0] - 3, na, nr), jnp.float32)
     lane = lax.broadcasted_iota(jnp.int32, (na, nr), 1)
     for f, held in enumerate(sources):
         flat = held.reshape(nt * na, nr)
         for side in range(2):
-            a_lo[f, side] = flat[pl.ds(side, nt, stride=na), :]
-            a_hi[f, side] = flat[pl.ds(na - 2 + side, nt, stride=na), :]
+            low = flat[pl.ds(side, nt, stride=na), :]
+            high = flat[pl.ds(na - 2 + side, nt, stride=na), :]
+            near[f, side] = jnp.where(even, high, low)
+            far[f, side] = jnp.where(even, low, high)
         shift = 4 * (f % 2)
         packed = r_pack[f // 2] if f % 2 else jnp.zeros((na, nr), jnp.float32)
         for t in range(nt):
             turn = (8 * t + shift) % nr
             x = held[t]
             turned = pltpu.roll(x, turn, 1) if turn else x
-            near = (lane + 2 - turn) % nr < 4
-            packed = jnp.where(near, turned, packed)
+            picked = (lane + 2 - turn) % nr < 4
+            packed = jnp.where(picked, turned, packed)
         r_pack[f // 2] = packed
 
 
@@ -78,16 +87,21 @@
 
 
 def fill(pad, halos, r_halo, keep):
-    s_lo, s_hi, a_lo, a_hi, r_left, r_right = halos
+    s_near, s_far, a_far, a_near, r_left, r_right = halos
     nt, na, nr = pad.shape[1] - 4, pad.shape[2] - 16, pad.shape[3]
     rows = na + 16
+    s_even, a_even = is_even("sector"), is_even("ax")
     for f in range(5):
-        pad[f, 0:2, 8 : 8 + na] = s_lo[f]
-        pad[f, nt + 2 : nt + 4, 8 : 8 + na] = s_hi[f]
-    for f in range(5):
+        pad[f, 0:2, 8 : 8 + na] = jnp.where(s_even, s_far[f], s_near[f])
+        pad[f, nt + 2 : nt + 4, 8 : 8 + na] = jnp.where(s_even, s_near[f], s_far[f])
         for side in range(2):
-            edge_rows(pad, f, 2 * rows + 6 + side, nt, rows)[...] = a_lo[f, side] * keep[0]
-            edge_rows(pad, f, 2 * rows + 8 + na + side, nt, rows)[...] = a_hi[f, side] * keep[1]
+            near, far = a_near[f, side], a_far[f, side]
+            edge_rows(pad, f, 2 * rows + 6 + side, nt, rows)[...] = (
+                jnp.where(a_even, far, near) * keep[0]
+            )
+            edge_rows(pad, f, 2 * rows + 8 + na + side, nt, rows)[...] = (
+                jnp.where(a_even, near, far) * keep[1]
+            )
     join_packs(r_halo, r_left, r_right, keep)
 
 
@@ -214,7 +228,7 @@
 
 
 def temperature_kernel(
-    vel, temp, base, s_lo, s_hi, a_lo, a_hi, r_left, r_right, cells, r_halo
+    vel, temp, base, s_near, s_far, a_far, a_near, r_left, r_right, cells, r_halo
 ):
     nt, na, nr = base.shape
     keep, rad, nrad = place()
@@ -222,6 +236,20 @@
     inv12h, gt, lane = spacings(rad, nrad, nr)
     inv12, g = 1.0 / 12.0, VISCOSITY / 12.0
     turned = cells.reshape(na * nt, nr)
+    s_even, a_even = is_even("sector"), is_even("ax")
+
+    def s_low(f, k, out):
+        return jnp.where(s_even, s_far[f, k, out], s_near[f, k, out])
+
+    def s_high(f, k, out):
+        return jnp.where(s_even, s_near[f, k, out], s_far[f, k, out])
+
+    def a_low(f, k):
+        return jnp.where(a_even, a_far[f, k], a_near[f, k])
+
+    def a_high(f, k):
+        return jnp.where(a_even, a_near[f, k], a_far[f, k])
+
     edge = (lane < 2) | (lane >= nr - 2)
     u_slope, _ = pack_parts(r_halo[1])
     t_slope, t_curve = pack_parts(r_halo[2])
@@ -237,10 +265,10 @@
             value = base[t, out] + jnp.where(edge, share, 0.0)
             parts = None
             if t < 2:
-                parts = [low_parts((s_lo[f, 0, out], s_lo[f, 1, out]), t) for f in (4, 1)]
+                parts = [low_parts([s_low(f, k, out) for k in (0, 1)], t) for f in (4, 1)]
             elif t >= nt - 2:
                 parts = [
-                    high_parts((s_hi[f, 0, out], s_hi[f, 1, out]), nt - 1 - t) for f in (4, 1)
+                    high_parts([s_high(f, k, out) for k in (0, 1)], nt - 1 - t) for f in (4, 1)
                 ]
             if parts is not None:
                 value = value + halo_share(mid, vel[0, t, out], inv12h, gt, *parts)
@@ -249,16 +277,16 @@
     for a in (0, 1, na - 2, na - 1):
         mid, u = rows[pl.ds(a, nt, stride=na), :], speeds[pl.ds(a, nt, stride=na), :]
         if a < 2:
-            parts = [low_parts((a_lo[f, 0], a_lo[f, 1]), a) for f in (4, 2)]
+            parts = [low_parts([a_low(f, k) for k in (0, 1)], a) for f in (4, 2)]
             scale = keep[0]
         else:
-            parts = [high_parts((a_hi[f, 0], a_hi[f, 1]), na - 1 - a) for f in (4, 2)]
+            parts = [high_parts([a_high(f, k) for k in (0, 1)], na - 1 - a) for f in (4, 2)]
             scale = keep[1]
         cells[a] = cells[a] + scale * halo_share(mid, u, inv12, g, *parts)
 
 
 def flow_kernel(
-    rho, vel, temp, cells, s_lo, s_hi, a_lo, a_hi, r_left, r_right,
+    rho, vel, temp, cells, s_near, s_far, a_far, a_near, r_left, r_right,
     new_rho, new_vel, new_temp,
     full, flux_t, flux_a, flux_r, press, r_halo,
 ):
@@ -266,7 +294,7 @@
     keep, rad, nrad = place()
     for f, ref in enumerate((rho, vel.at[0], vel.at[1], vel.at[2], temp)):
         full[f, 2 : nt + 2, 8 : 8 + na] = ref[...]
-    halos = (s_lo, s_hi, a_lo, a_hi, r_left, r_right)
+    halos = (s_near, s_far, a_far, a_near, r_left, r_right)
     fill(full, halos, r_halo, keep)
 
     def products(t, carry):
@@ -362,7 +390,7 @@
     hbm = pl.BlockSpec(memory_space=pltpu.HBM)
     vmem = pl.BlockSpec(memory_space=pltpu.VMEM)
     padded = (nt + 4, na + 16, nr)
-    s_lo, s_hi = pl.pallas_call(
+    s_far, s_near = pl.pallas_call(
         sector_edges_kernel,
         in_specs=[hbm] * 3,
         out_specs=[vmem] * 2,
@@ -371,7 +399,7 @@
         compiler_params=pltpu.CompilerParams(vmem_limit_bytes=54912 * 1024),
         name="sector_edges",
     )(mass_excess, speed_vector, thermal_excess)
-    a_lo, a_hi, r_pack = pl.pallas_call(
+    a_near, a_far, r_pack = pl.pallas_call(
         tile_edges_kernel,
         in_specs=[vmem] * 4,
         out_specs=[vmem] * 3,
@@ -382,20 +410,23 @@
         ),
         compiler_params=params,
         name="tile_edges",
-    )(s_lo, mass_excess, speed_vector, thermal_excess)
+    )(s_far, mass_excess, speed_vector, thermal_excess)
 
     def ring(axis, up):
         count = lax.axis_size(axis)
         return [(i, (i + (1 if up else -1)) % count) for i in range(count)]
 
-    halos = (
-        lax.ppermute(s_hi, "sector", ring("sector", True)),
-        lax.ppermute(s_lo, "sector", ring("sector", False)),
-        lax.ppermute(a_hi, "ax", ring("ax", True)),
-        lax.ppermute(a_lo, "ax", ring("ax", False)),
-        lax.ppermute(r_pack, "rad", ring("rad", True)),
-        lax.ppermute(r_pack, "rad", ring("rad", False)),
-    )
+    def pairs(axis, near):
+        count = lax.axis_size(axis)
+        return [(i, i ^ 1 if near else (i + (1 if i % 2 else -1)) % count) for i in range(count)]
+
+    s_near = lax.ppermute(s_near, "sector", pairs("sector", True))
+    s_far = lax.ppermute(s_far, "sector", pairs("sector", False))
+    a_far = lax.ppermute(a_far, "ax", pairs("ax", False))
+    a_near = lax.ppermute(a_near, "ax", pairs("ax", True))
+    r_left = lax.ppermute(r_pack, "rad", ring("rad", True))
+    r_right = lax.ppermute(r_pack, "rad", ring("rad", False))
+    halos = (s_near, s_far, a_far, a_near, r_left, r_right)
     (base,) = pl.pallas_call(
         inner_kernel,
         in_specs=[vmem] * 3,

time: 49.2 us -> 47.4 us (0.963); the launches traced: 48.5 us -> 47.2 us
  starting transfers between devices: 17.4 us -> 15.3 us
  waiting for transfers between devices: 5.46 us -> 6.48 us
    ppermute x6, starting transfers between devices: 12 us -> 10.7 us  [the longest x1 5.97 us: per_device(): s_far = lax.ppermute(s_far, 'sector', pairs('sector', False))]
    ppermute x6, waiting for transfers between devices: 2.03 us -> 3.22 us  [the longest x1 1.82 us: per_device(): r_left = lax.ppermute(r_pack, 'rad', ring('rad', True))]
    all_to_all x1, starting transfers between devices: 5.46 us -> 4.54 us  [per_device(): terms = lax.all_to_all(terms, 'sector', 0, 0, tiled=True)]
  transfers between devices with their start and end apart: 7 -> 7, of which waited for: 2 -> 4; matrix products, arithmetic and copies ran while one was open for 0% -> 0% of each run, Pallas kernels for 14% -> 14%
where the time goes in v4:
time: 47.4 us; the launch traced here: 47.2 us
  starting transfers between devices  15.3 us (32%)
  blocking collectives  14.2 us (30%)
  Pallas kernels  10.2 us (22%)
  waiting for transfers between devices  6.48 us (14%)
  between operations  0.73 us (2%)
    all_to_all x1, blocking collectives, per_device(): lax.all_to_all(cells.reshape(sectors, share, nt, nr), 'sector', 0, 0, til...  14.2 us
    ppermute x1, starting transfers between devices, per_device(): s_far = lax.ppermute(s_far, 'sector', pairs('sector', False))  5.97 us
    pallas_call x1, Pallas kernels, per_device(): pl.pallas_call(flow_kernel, in_specs=[vmem] * 10, out_shape=(sds((nt, na,...  5.32 us
    all_to_all x1, starting transfers between devices, per_device(): terms = lax.all_to_all(terms, 'sector', 0, 0, tiled=True)  4.54 us
    all_to_all x1, waiting for transfers between devices, per_device(): terms = lax.all_to_all(terms, 'sector', 0, 0, tiled=True)  3.26 us
    ppermute x1, starting transfers between devices, per_device(): a_far = lax.ppermute(a_far, 'ax', pairs('ax', False))  2.72 us
    ppermute x1, waiting for transfers between devices, per_device(): r_left = lax.ppermute(r_pack, 'rad', ring('rad', True))  1.82 us
    ppermute x1, starting transfers between devices, per_device(): r_left = lax.ppermute(r_pack, 'rad', ring('rad', True))  1.49 us
  transfers between devices with their start and end apart: 7, of which 4 were waited for; matrix products, arithmetic and copies ran while one was open for 0% of the time, Pallas kernels for 14%

profile of v4, /device:TPU:2, one launch (start us, length us, event | category | flops | bytes accessed | tf_op | source)
XLA Modules:
  0.0 47.2 jit_solution(18107587803319956035)
XLA Ops:
  0.7 1.1 %sector_edges.1 = (f32[5,2,32,128]{3,2,1,0:T(8,128)S(1)}, f32[5,2,32,128]{3,2,1,0:T(8,128)S(1)}) custom-call(f32[16,32,128]{2,1,0:T(8,128)} %rho.5, f32[3,16,32,128]{3,2,1,0:T(8,128)} %vel.9, f32[16,32,128]{2,1,0:T(8,128)} %temp.9), custom_call_target="tpu_custom_call" | custom-call | tf_op jit(solution)/shard_map/sector_edges/pallas_call | solution.py:393
  1.8 0.2 copy-done
  2.0 0.0 copy-done.1
  2.1 0.4 tile_edges.1
  2.5 2.7 %collective-permute-start.2 = (f32[5,2,16,128]{3,2,1,0:T(8,128)S(1)}, f32[5,2,16,128]{3,2,1,0:T(8,128)S(1)}, u32[]{:S(2)}, u32[]{:S(2)}) collective-permute-start(f32[5,2,16,128]{3,2,1,0:T(8,128)S(1)} %get-tuple-element.14), channel_id=1, source_target_pairs={{0,12},{4,8},{8,4},{12,0},{1,13},{5,9},{9,5},{13,1},{2,14},{6,10},... | collective-permute-start | bytes 245768 | tf_op jit(solution)/shard_map/ppermute | solution.py:425
  5.2 6.0 %collective-permute-start.1 = (f32[5,2,32,128]{3,2,1,0:T(8,128)S(1)}, f32[5,2,32,128]{3,2,1,0:T(8,128)S(1)}, u32[]{:S(2)}, u32[]{:S(2)}) collective-permute-start(f32[5,2,32,128]{3,2,1,0:T(8,128)S(1)} %get-tuple-element.13.after), channel_id=1, source_target_pairs={{0,240},{16,32},{32,16},{48,64},{64,48},{80,96},{96,80},{112,128},... | collective-permute-start | bytes 491528 | tf_op jit(solution)/shard_map/ppermute | solution.py:424
  11.2 0.0 collective-permute-start
  11.2 1.5 %collective-permute-start.4 = (f32[6,32,128]{2,1,0:T(8,128)S(1)}, f32[6,32,128]{2,1,0:T(8,128)S(1)}, u32[]{:S(2)}, u32[]{:S(2)}) collective-permute-start(f32[6,32,128]{2,1,0:T(8,128)S(1)} %get-tuple-element.16), channel_id=1, source_target_pairs={{0,1},{1,2},{2,3},{3,0},{4,5},{5,6},{6,7},{7,4},{8,9},{9,10},{10,1... | collective-permute-start | bytes 294920 | tf_op jit(solution)/shard_map/ppermute | solution.py:427
  12.7 0.5 %collective-permute-start.5 = (f32[6,32,128]{2,1,0:T(8,128)S(1)}, f32[6,32,128]{2,1,0:T(8,128)S(1)}, u32[]{:S(2)}, u32[]{:S(2)}) collective-permute-start(f32[6,32,128]{2,1,0:T(8,128)S(1)} %get-tuple-element.16), channel_id=1, source_target_pairs={{0,3},{1,0},{2,1},{3,2},{4,7},{5,4},{6,5},{7,6},{8,11},{9,8},{10,9... | collective-permute-start | bytes 294920 | tf_op jit(solution)/shard_map/ppermute | solution.py:428
  13.2 0.0 collective-permute-done.2.a_far
  13.2 0.0 collective-permute-start.3
  13.2 1.3 %inner.1.base = f32[16,32,128]{2,1,0:T(8,128)S(1)} custom-call(f32[3,16,32,128]{3,2,1,0:T(8,128)S(1)} %copy-done, f32[16,32,128]{2,1,0:T(8,128)S(1)} %copy-done.1, f32[16,32,128]{2,1,0:T(8,128)S(1)} %copy-done.3), custom_call_target="tpu_custom_call" | custom-call | flops 5242880 | bytes 1572864 | tf_op jit(solution)/shard_map/inner/pallas_call | solution.py:430
  14.5 0.0 collective-permute-done.3.a_near
  14.5 1.8 %collective-permute-done.4.r_left = f32[6,32,128]{2,1,0:T(8,128)S(1)} collective-permute-done((f32[6,32,128]{2,1,0:T(8,128)S(1)}, f32[6,32,128]{2,1,0:T(8,128)S(1)}, u32[]{:S(2)}, u32[]{:S(2)}) %collective-permute-start.4) | collective-permute-done | bytes 98336 | tf_op jit(solution)/shard_map/ppermute | solution.py:427
  16.3 1.2 %collective-permute-done.5.r_right = f32[6,32,128]{2,1,0:T(8,128)S(1)} collective-permute-done((f32[6,32,128]{2,1,0:T(8,128)S(1)}, f32[6,32,128]{2,1,0:T(8,128)S(1)}, u32[]{:S(2)}, u32[]{:S(2)}) %collective-permute-start.5) | collective-permute-done | bytes 98336 | tf_op jit(solution)/shard_map/ppermute | solution.py:428
  17.5 0.2 collective-permute-done.s_near
  17.7 0.4 temperature.1.cells
  18.1 0.0 copy-start.4
  18.2 14.2 %all_to_all.10.spread = f32[16,2,16,128]{3,2,1,0:T(8,128)S(1)} all-to-all(f32[16,2,16,128]{3,2,1,0:T(8,128)S(1)} %bitcast.2), channel_id=1, replica_groups=mesh['sector'=16,'ax'=4,'rad'=4] {'sector'}, dimensions={0} | all-to-all | bytes 524288 | tf_op jit(solution)/shard_map/all_to_all | solution.py:454
  32.4 1.0 %harmonics.1 = f32[16,2,8,128]{3,2,1,0:T(8,128)} custom-call(f32[128,256]{1,0:T(8,128)S(1)} %copy-done.4, f32[16,2,16,128]{3,2,1,0:T(8,128)S(1)} %all_to_all.10.spread), custom_call_target="tpu_custom_call" | custom-call | tf_op jit(solution)/shard_map/harmonics/pallas_call | solution.py:479
  33.4 4.5 %all-to-all-start.1 = ((f32[16,2,8,128]{3,2,1,0:T(8,128)}), f32[16,2,8,128]{3,2,1,0:T(8,128)S(1)}, u32[]{:S(2)}, u32[]{:S(2)}) async-start(f32[16,2,8,128]{3,2,1,0:T(8,128)} %harmonics.1), calls=%async_computation.1 | async-start | bytes 262144 | tf_op jit(solution)/shard_map/all_to_all | solution.py:491
  37.9 5.3 %flow.1 = (f32[16,32,128]{2,1,0:T(8,128)}, f32[3,16,32,128]{3,2,1,0:T(8,128)}, f32[16,32,128]{2,1,0:T(8,128)}) custom-call(f32[16,32,128]{2,1,0:T(8,128)S(1)} %copy-done.2, f32[3,16,32,128]{3,2,1,0:T(8,128)S(1)} %copy-done, f32[16,32,128]{2,1,0:T(8,128)S(1)} %copy-done.1, f32[32,16,128]{2,1,0:T(8,128)S(1)} %temperature.1.cells, ...), custom_call_target="tpu_custom_call" | custom-call | flops 11796480 | bytes 2883584 | tf_op jit(solution)/shard_map/flow/pallas_call | solution.py:457
  43.3 3.3 %all-to-all-done.1 = f32[16,2,8,128]{3,2,1,0:T(8,128)S(1)} async-done(((f32[16,2,8,128]{3,2,1,0:T(8,128)}), f32[16,2,8,128]{3,2,1,0:T(8,128)S(1)}, u32[]{:S(2)}, u32[]{:S(2)}) %all-to-all-start.1) | async-done | bytes 131104 | tf_op jit(solution)/shard_map/all_to_all | solution.py:491
  46.5 0.7 %gather.1 = f32[8,32,128]{2,1,0:T(8,128)} custom-call(f32[32,8,128]{2,1,0:T(8,128)S(1)} %bitcast.3), custom_call_target="tpu_custom_call" | custom-call | tf_op jit(solution)/shard_map/gather/pallas_call | solution.py:492
  (8 shorter events, 0.0 us)
Async XLA Ops:
  0.6 1.1 %copy-start.2 = (f32[16,32,128]{2,1,0:T(8,128)S(1)}, f32[16,32,128]{2,1,0:T(8,128)}, u32[]{:S(2)}) copy-start(f32[16,32,128]{2,1,0:T(8,128)} %rho.5) | copy-start | bytes 786436
  0.6 1.4 %copy-start = (f32[3,16,32,128]{3,2,1,0:T(8,128)S(1)}, f32[3,16,32,128]{3,2,1,0:T(8,128)}, u32[]{:S(2)}) copy-start(f32[3,16,32,128]{3,2,1,0:T(8,128)} %vel.9) | copy-start | bytes 2359300
  0.7 1.4 %copy-start.1 = (f32[16,32,128]{2,1,0:T(8,128)S(1)}, f32[16,32,128]{2,1,0:T(8,128)}, u32[]{:S(2)}) copy-start(f32[16,32,128]{2,1,0:T(8,128)} %temp.9) | copy-start | bytes 786436
  2.1 11.2 %copy-start.3 = (f32[16,32,128]{2,1,0:T(8,128)S(1)}, f32[16,32,128]{2,1,0:T(8,128)}, u32[]{:S(2)}) copy-start(f32[16,32,128]{2,1,0:T(8,128)} %heat.1) | copy-start | bytes 786436
  2.5 10.7 %collective-permute-start.2 = (f32[5,2,16,128]{3,2,1,0:T(8,128)S(1)}, f32[5,2,16,128]{3,2,1,0:T(8,128)S(1)}, u32[]{:S(2)}, u32[]{:S(2)}) collective-permute-start(f32[5,2,16,128]{3,2,1,0:T(8,128)S(1)} %get-tuple-element.14), channel_id=1, source_target_pairs={{0,12},{4,8},{8,4},{12,0},{1,13},{5,9},{9,5},{13,1},{2,14},{6,10},... | collective-permute-start | bytes 245768 | tf_op jit(solution)/shard_map/ppermute | solution.py:425
  5.2 12.3 %collective-permute-start.1 = (f32[5,2,32,128]{3,2,1,0:T(8,128)S(1)}, f32[5,2,32,128]{3,2,1,0:T(8,128)S(1)}, u32[]{:S(2)}, u32[]{:S(2)}) collective-permute-start(f32[5,2,32,128]{3,2,1,0:T(8,128)S(1)} %get-tuple-element.13.after), channel_id=1, source_target_pairs={{0,240},{16,32},{32,16},{48,64},{64,48},{80,96},{96,80},{112,128},... | collective-permute-start | bytes 491528 | tf_op jit(solution)/shard_map/ppermute | solution.py:424
  11.2 6.5 %collective-permute-start = (f32[5,2,32,128]{3,2,1,0:T(8,128)S(1)}, f32[5,2,32,128]{3,2,1,0:T(8,128)S(1)}, u32[]{:S(2)}, u32[]{:S(2)}) collective-permute-start(f32[5,2,32,128]{3,2,1,0:T(8,128)S(1)} %get-tuple-element.12), channel_id=1, source_target_pairs={{0,16},{16,0},{32,48},{48,32},{64,80},{80,64},{96,112},{112,96},{1... | collective-permute-start | bytes 491528 | tf_op jit(solution)/shard_map/ppermute | solution.py:423
  11.2 5.1 %collective-permute-start.4 = (f32[6,32,128]{2,1,0:T(8,128)S(1)}, f32[6,32,128]{2,1,0:T(8,128)S(1)}, u32[]{:S(2)}, u32[]{:S(2)}) collective-permute-start(f32[6,32,128]{2,1,0:T(8,128)S(1)} %get-tuple-element.16), channel_id=1, source_target_pairs={{0,1},{1,2},{2,3},{3,0},{4,5},{5,6},{6,7},{7,4},{8,9},{9,10},{10,1... | collective-permute-start | bytes 294920 | tf_op jit(solution)/shard_map/ppermute | solution.py:427
  12.7 4.8 %collective-permute-start.5 = (f32[6,32,128]{2,1,0:T(8,128)S(1)}, f32[6,32,128]{2,1,0:T(8,128)S(1)}, u32[]{:S(2)}, u32[]{:S(2)}) collective-permute-start(f32[6,32,128]{2,1,0:T(8,128)S(1)} %get-tuple-element.16), channel_id=1, source_target_pairs={{0,3},{1,0},{2,1},{3,2},{4,7},{5,4},{6,5},{7,6},{8,11},{9,8},{10,9... | collective-permute-start | bytes 294920 | tf_op jit(solution)/shard_map/ppermute | solution.py:428
  13.2 1.3 %collective-permute-start.3 = (f32[5,2,16,128]{3,2,1,0:T(8,128)S(1)}, f32[5,2,16,128]{3,2,1,0:T(8,128)S(1)}, u32[]{:S(2)}, u32[]{:S(2)}) collective-permute-start(f32[5,2,16,128]{3,2,1,0:T(8,128)S(1)} %get-tuple-element.15), channel_id=1, source_target_pairs={{0,4},{4,0},{8,12},{12,8},{1,5},{5,1},{9,13},{13,9},{2,6},{6,2},{1... | collective-permute-start | bytes 245768 | tf_op jit(solution)/shard_map/ppermute | solution.py:426
  18.1 14.2 %copy-start.4 = (f32[128,256]{1,0:T(8,128)S(1)}, f32[128,256]{1,0:T(8,128)}, u32[]{:S(2)}) copy-start(f32[128,256]{1,0:T(8,128)} %constant.2.clone.table) | copy-start | bytes 393220
  33.4 13.1 %all-to-all-start.1 = ((f32[16,2,8,128]{3,2,1,0:T(8,128)}), f32[16,2,8,128]{3,2,1,0:T(8,128)S(1)}, u32[]{:S(2)}, u32[]{:S(2)}) async-start(f32[16,2,8,128]{3,2,1,0:T(8,128)} %harmonics.1), calls=%async_computation.1 | async-start | bytes 262144 | tf_op jit(solution)/shard_map/all_to_all | solution.py:491

commit v5 on v4

--- a/solution.py
+++ b/solution.py
@@ -52,12 +52,14 @@
         copy.wait()
 
 
-def tile_edges_kernel(after, rho, vel, temp, near, far, r_pack):
+def tile_edges_kernel(after, rho, vel, temp, near, far, r_pack, r_copy):
     del after
     nt, na, nr = rho.shape
     sources = [rho, vel.at[0], vel.at[1], vel.at[2], temp]
     even = is_even("ax")
-    r_pack[3:] = jnp.zeros((r_pack.shape[0] - 3, na, nr), jnp.float32)
+    for ref in (r_pack, r_copy):
+        if ref.shape[0] > 3:
+            ref[3:] = jnp.zeros((ref.shape[0] - 3, na, nr), jnp.float32)
     lane = lax.broadcasted_iota(jnp.int32, (na, nr), 1)
     for f, held in enumerate(sources):
         flat = held.reshape(nt * na, nr)
@@ -75,6 +77,7 @@
             picked = (lane + 2 - turn) % nr < 4
             packed = jnp.where(picked, turned, packed)
         r_pack[f // 2] = packed
+        r_copy[f // 2] = packed
 
 
 def place():
@@ -87,7 +90,7 @@
 
 
 def fill(pad, halos, r_halo, keep):
-    s_near, s_far, a_far, a_near, r_left, r_right = halos
+    s_near, s_far, a_far, a_near, r_right, r_left = halos
     nt, na, nr = pad.shape[1] - 4, pad.shape[2] - 16, pad.shape[3]
     rows = na + 16
     s_even, a_even = is_even("sector"), is_even("ax")
@@ -228,7 +231,7 @@
 
 
 def temperature_kernel(
-    vel, temp, base, s_near, s_far, a_far, a_near, r_left, r_right, cells, r_halo
+    vel, temp, base, s_near, s_far, a_far, a_near, r_right, r_left, cells, r_halo
 ):
     nt, na, nr = base.shape
     keep, rad, nrad = place()
@@ -286,7 +289,7 @@
 
 
 def flow_kernel(
-    rho, vel, temp, cells, s_near, s_far, a_far, a_near, r_left, r_right,
+    rho, vel, temp, cells, s_near, s_far, a_far, a_near, r_right, r_left,
     new_rho, new_vel, new_temp,
     full, flux_t, flux_a, flux_r, press, r_halo,
 ):
@@ -294,7 +297,7 @@
     keep, rad, nrad = place()
     for f, ref in enumerate((rho, vel.at[0], vel.at[1], vel.at[2], temp)):
         full[f, 2 : nt + 2, 8 : 8 + na] = ref[...]
-    halos = (s_near, s_far, a_far, a_near, r_left, r_right)
+    halos = (s_near, s_far, a_far, a_near, r_right, r_left)
     fill(full, halos, r_halo, keep)
 
     def products(t, carry):
@@ -399,13 +402,14 @@
         compiler_params=pltpu.CompilerParams(vmem_limit_bytes=54912 * 1024),
         name="sector_edges",
     )(mass_excess, speed_vector, thermal_excess)
-    a_near, a_far, r_pack = pl.pallas_call(
+    a_near, a_far, r_pack, r_copy = pl.pallas_call(
         tile_edges_kernel,
         in_specs=[vmem] * 4,
-        out_specs=[vmem] * 3,
+        out_specs=[vmem] * 4,
         out_shape=(
             sds((5, 2, nt, nr), f32),
             sds((5, 2, nt, nr), f32),
+            sds((3, na, nr), f32),
             sds((PACK_PLANES, na, nr), f32),
         ),
         compiler_params=params,
@@ -425,8 +429,8 @@
     a_far = lax.ppermute(a_far, "ax", pairs("ax", False))
     a_near = lax.ppermute(a_near, "ax", pairs("ax", True))
     r_left = lax.ppermute(r_pack, "rad", ring("rad", True))
-    r_right = lax.ppermute(r_pack, "rad", ring("rad", False))
-    halos = (s_near, s_far, a_far, a_near, r_left, r_right)
+    r_right = lax.ppermute(r_copy, "rad", ring("rad", False))
+    halos = (s_near, s_far, a_far, a_near, r_right, r_left)
     (base,) = pl.pallas_call(
         inner_kernel,
         in_specs=[vmem] * 3,

time: 47.4 us -> 47.4 us (level)
  waiting for transfers between devices: 6.48 us -> 5.74 us
  starting transfers between devices: 15.3 us -> 16 us
    ppermute x1, waiting for transfers between devices: 0.01 us -> 1.91 us  [per_device(): a_far = lax.ppermute(a_far, 'ax', pairs('ax', False))]
    ppermute x1, waiting for transfers between devices: 1.82 us -> 0.56 us  [per_device(): r_left = lax.ppermute(r_pack, 'rad', ring('rad', True))]
    ppermute x1, starting transfers between devices: 2.72 us -> 1.5 us  [per_device(): a_far = lax.ppermute(a_far, 'ax', pairs('ax', False))]
    ppermute x1, waiting for transfers between devices: 1.21 us -> 0.01 us  [per_device(): r_right = lax.ppermute(r_copy, 'rad', ring('rad', False))]
    ppermute x1, starting transfers between devices: 5.97 us -> 6.96 us  [per_device(): s_far = lax.ppermute(s_far, 'sector', pairs('sector', False))]
    ppermute x1, starting transfers between devices: 0.01 us -> 0.96 us  [per_device(): a_near = lax.ppermute(a_near, 'ax', pairs('ax', True))]
  transfers between devices with their start and end apart: 7 -> 7, of which waited for: 4 -> 3; matrix products, arithmetic and copies ran while one was open for 0% -> 0% of each run, Pallas kernels for 14% -> 15%
where the time goes in v5:
time: 47.4 us; the launch traced here: 46.9 us
  starting transfers between devices  16 us (34%)
  blocking collectives  14.2 us (30%)
  Pallas kernels  10.2 us (22%)
  waiting for transfers between devices  5.74 us (12%)
  between operations  0.74 us (2%)
    all_to_all x1, blocking collectives, per_device(): lax.all_to_all(cells.reshape(sectors, share, nt, nr), 'sector', 0, 0, til...  14.2 us
    ppermute x1, starting transfers between devices, per_device(): s_far = lax.ppermute(s_far, 'sector', pairs('sector', False))  6.96 us
    pallas_call x1, Pallas kernels, per_device(): pl.pallas_call(flow_kernel, in_specs=[vmem] * 10, out_shape=(sds((nt, na,...  5.32 us
    all_to_all x1, starting transfers between devices, per_device(): terms = lax.all_to_all(terms, 'sector', 0, 0, tiled=True)  4.52 us
    all_to_all x1, waiting for transfers between devices, per_device(): terms = lax.all_to_all(terms, 'sector', 0, 0, tiled=True)  3.26 us
    ppermute x1, waiting for transfers between devices, per_device(): a_far = lax.ppermute(a_far, 'ax', pairs('ax', False))  1.91 us
    ppermute x1, starting transfers between devices, per_device(): r_left = lax.ppermute(r_pack, 'rad', ring('rad', True))  1.57 us
    ppermute x1, starting transfers between devices, per_device(): a_far = lax.ppermute(a_far, 'ax', pairs('ax', False))  1.5 us
  transfers between devices with their start and end apart: 7, of which 3 were waited for; matrix products, arithmetic and copies ran while one was open for 0% of the time, Pallas kernels for 15%

profile of v5, /device:TPU:2, one launch (start us, length us, event | category | flops | bytes accessed | tf_op | source)
XLA Modules:
  0.0 46.9 jit_solution(12871890851941572520)
XLA Ops:
  0.6 0.0 copy-start.2
  0.7 1.1 %sector_edges.1 = (f32[5,2,32,128]{3,2,1,0:T(8,128)S(1)}, f32[5,2,32,128]{3,2,1,0:T(8,128)S(1)}) custom-call(f32[16,32,128]{2,1,0:T(8,128)} %rho.5, f32[3,16,32,128]{3,2,1,0:T(8,128)} %vel.9, f32[16,32,128]{2,1,0:T(8,128)} %temp.9), custom_call_target="tpu_custom_call" | custom-call | tf_op jit(solution)/shard_map/sector_edges/pallas_call | solution.py:396
  1.8 7.0 %collective-permute-start.1 = (f32[5,2,32,128]{3,2,1,0:T(8,128)S(1)}, f32[5,2,32,128]{3,2,1,0:T(8,128)S(1)}, u32[]{:S(2)}, u32[]{:S(2)}) collective-permute-start(f32[5,2,32,128]{3,2,1,0:T(8,128)S(1)} %get-tuple-element.14.after), channel_id=1, source_target_pairs={{0,240},{16,32},{32,16},{48,64},{64,48},{80,96},{96,80},{112,128},... | collective-permute-start | bytes 491528 | tf_op jit(solution)/shard_map/ppermute | solution.py:428
  8.7 0.0 collective-permute-start
  8.7 0.4 tile_edges.1
  9.2 1.6 %collective-permute-start.5 = (f32[3,32,128]{2,1,0:T(8,128)S(1)}, f32[3,32,128]{2,1,0:T(8,128)S(1)}, u32[]{:S(2)}, u32[]{:S(2)}) collective-permute-start(f32[3,32,128]{2,1,0:T(8,128)S(1)} %get-tuple-element.18), channel_id=1, source_target_pairs={{0,1},{1,2},{2,3},{3,0},{4,5},{5,6},{6,7},{7,4},{8,9},{9,10},{10,1... | collective-permute-start | bytes 147464 | tf_op jit(solution)/shard_map/ppermute | solution.py:431
  10.8 0.5 %collective-permute-start.4 = (f32[6,32,128]{2,1,0:T(8,128)S(1)}, f32[6,32,128]{2,1,0:T(8,128)S(1)}, u32[]{:S(2)}, u32[]{:S(2)}) collective-permute-start(f32[6,32,128]{2,1,0:T(8,128)S(1)} %get-tuple-element.17), channel_id=1, source_target_pairs={{0,3},{1,0},{2,1},{3,2},{4,7},{5,4},{6,5},{7,6},{8,11},{9,8},{10,9... | collective-permute-start | bytes 294920 | tf_op jit(solution)/shard_map/ppermute | solution.py:432
  11.3 1.5 %collective-permute-start.2 = (f32[5,2,16,128]{3,2,1,0:T(8,128)S(1)}, f32[5,2,16,128]{3,2,1,0:T(8,128)S(1)}, u32[]{:S(2)}, u32[]{:S(2)}) collective-permute-start(f32[5,2,16,128]{3,2,1,0:T(8,128)S(1)} %get-tuple-element.15), channel_id=1, source_target_pairs={{0,12},{4,8},{8,4},{12,0},{1,13},{5,9},{9,5},{13,1},{2,14},{6,10},... | collective-permute-start | bytes 245768 | tf_op jit(solution)/shard_map/ppermute | solution.py:429
  12.8 0.6 %collective-permute-done.5.r_left = f32[3,32,128]{2,1,0:T(8,128)S(1)} collective-permute-done((f32[3,32,128]{2,1,0:T(8,128)S(1)}, f32[3,32,128]{2,1,0:T(8,128)S(1)}, u32[]{:S(2)}, u32[]{:S(2)}) %collective-permute-start.5) | collective-permute-done | bytes 49184 | tf_op jit(solution)/shard_map/ppermute | solution.py:431
  13.4 1.0 %collective-permute-start.3 = (f32[5,2,16,128]{3,2,1,0:T(8,128)S(1)}, f32[5,2,16,128]{3,2,1,0:T(8,128)S(1)}, u32[]{:S(2)}, u32[]{:S(2)}) collective-permute-start(f32[5,2,16,128]{3,2,1,0:T(8,128)S(1)} %get-tuple-element.16), channel_id=1, source_target_pairs={{0,4},{4,0},{8,12},{12,8},{1,5},{5,1},{9,13},{13,9},{2,6},{6,2},{1... | collective-permute-start | bytes 245768 | tf_op jit(solution)/shard_map/ppermute | solution.py:430
  14.3 1.3 %inner.1.base = f32[16,32,128]{2,1,0:T(8,128)S(1)} custom-call(f32[3,16,32,128]{3,2,1,0:T(8,128)S(1)} %copy-done, f32[16,32,128]{2,1,0:T(8,128)S(1)} %copy-done.1, f32[16,32,128]{2,1,0:T(8,128)S(1)} %copy-done.3), custom_call_target="tpu_custom_call" | custom-call | flops 5242880 | bytes 1572864 | tf_op jit(solution)/shard_map/inner/pallas_call | solution.py:434
  15.6 1.9 %collective-permute-done.2.a_far = f32[5,2,16,128]{3,2,1,0:T(8,128)S(1)} collective-permute-done((f32[5,2,16,128]{3,2,1,0:T(8,128)S(1)}, f32[5,2,16,128]{3,2,1,0:T(8,128)S(1)}, u32[]{:S(2)}, u32[]{:S(2)}) %collective-permute-start.2) | collective-permute-done | bytes 81952 | tf_op jit(solution)/shard_map/ppermute | solution.py:429
  17.5 0.0 collective-permute-done.3.a_near
  17.5 0.0 collective-permute-done.4.r_right
  17.5 0.0 collective-permute-done.1.s_far
  17.5 0.0 collective-permute-done.s_near
  17.5 0.4 temperature.1.cells
  17.9 0.0 copy-start.4
  18.0 14.2 %all_to_all.10.spread = f32[16,2,16,128]{3,2,1,0:T(8,128)S(1)} all-to-all(f32[16,2,16,128]{3,2,1,0:T(8,128)S(1)} %bitcast.2), channel_id=1, replica_groups=mesh['sector'=16,'ax'=4,'rad'=4] {'sector'}, dimensions={0} | all-to-all | bytes 524288 | tf_op jit(solution)/shard_map/all_to_all | solution.py:458
  32.1 1.0 %harmonics.1 = f32[16,2,8,128]{3,2,1,0:T(8,128)} custom-call(f32[128,256]{1,0:T(8,128)S(1)} %copy-done.4, f32[16,2,16,128]{3,2,1,0:T(8,128)S(1)} %all_to_all.10.spread), custom_call_target="tpu_custom_call" | custom-call | tf_op jit(solution)/shard_map/harmonics/pallas_call | solution.py:483
  33.2 4.5 %all-to-all-start.1 = ((f32[16,2,8,128]{3,2,1,0:T(8,128)}), f32[16,2,8,128]{3,2,1,0:T(8,128)S(1)}, u32[]{:S(2)}, u32[]{:S(2)}) async-start(f32[16,2,8,128]{3,2,1,0:T(8,128)} %harmonics.1), calls=%async_computation.1 | async-start | bytes 262144 | tf_op jit(solution)/shard_map/all_to_all | solution.py:495
  37.7 5.3 %flow.1 = (f32[16,32,128]{2,1,0:T(8,128)}, f32[3,16,32,128]{3,2,1,0:T(8,128)}, f32[16,32,128]{2,1,0:T(8,128)}) custom-call(f32[16,32,128]{2,1,0:T(8,128)S(1)} %copy-done.2, f32[3,16,32,128]{3,2,1,0:T(8,128)S(1)} %copy-done, f32[16,32,128]{2,1,0:T(8,128)S(1)} %copy-done.1, f32[32,16,128]{2,1,0:T(8,128)S(1)} %temperature.1.cells, ...), custom_call_target="tpu_custom_call" | custom-call | flops 11796480 | bytes 2883584 | tf_op jit(solution)/shard_map/flow/pallas_call | solution.py:461
  43.0 3.3 %all-to-all-done.1 = f32[16,2,8,128]{3,2,1,0:T(8,128)S(1)} async-done(((f32[16,2,8,128]{3,2,1,0:T(8,128)}), f32[16,2,8,128]{3,2,1,0:T(8,128)S(1)}, u32[]{:S(2)}, u32[]{:S(2)}) %all-to-all-start.1) | async-done | bytes 131104 | tf_op jit(solution)/shard_map/all_to_all | solution.py:495
  46.3 0.7 %gather.1 = f32[8,32,128]{2,1,0:T(8,128)} custom-call(f32[32,8,128]{2,1,0:T(8,128)S(1)} %bitcast.3), custom_call_target="tpu_custom_call" | custom-call | tf_op jit(solution)/shard_map/gather/pallas_call | solution.py:496
  (8 shorter events, 0.0 us)
Async XLA Ops:
  0.6 8.1 %copy-start.2 = (f32[16,32,128]{2,1,0:T(8,128)S(1)}, f32[16,32,128]{2,1,0:T(8,128)}, u32[]{:S(2)}) copy-start(f32[16,32,128]{2,1,0:T(8,128)} %rho.5) | copy-start | bytes 786436
  0.6 8.1 %copy-start = (f32[3,16,32,128]{3,2,1,0:T(8,128)S(1)}, f32[3,16,32,128]{3,2,1,0:T(8,128)}, u32[]{:S(2)}) copy-start(f32[3,16,32,128]{3,2,1,0:T(8,128)} %vel.9) | copy-start | bytes 2359300
  0.7 8.1 %copy-start.1 = (f32[16,32,128]{2,1,0:T(8,128)S(1)}, f32[16,32,128]{2,1,0:T(8,128)}, u32[]{:S(2)}) copy-start(f32[16,32,128]{2,1,0:T(8,128)} %temp.9) | copy-start | bytes 786436
  1.8 15.7 %collective-permute-start.1 = (f32[5,2,32,128]{3,2,1,0:T(8,128)S(1)}, f32[5,2,32,128]{3,2,1,0:T(8,128)S(1)}, u32[]{:S(2)}, u32[]{:S(2)}) collective-permute-start(f32[5,2,32,128]{3,2,1,0:T(8,128)S(1)} %get-tuple-element.14.after), channel_id=1, source_target_pairs={{0,240},{16,32},{32,16},{48,64},{64,48},{80,96},{96,80},{112,128},... | collective-permute-start | bytes 491528 | tf_op jit(solution)/shard_map/ppermute | solution.py:428
  8.7 5.6 %copy-start.3 = (f32[16,32,128]{2,1,0:T(8,128)S(1)}, f32[16,32,128]{2,1,0:T(8,128)}, u32[]{:S(2)}) copy-start(f32[16,32,128]{2,1,0:T(8,128)} %heat.1) | copy-start | bytes 786436
  8.7 8.8 %collective-permute-start = (f32[5,2,32,128]{3,2,1,0:T(8,128)S(1)}, f32[5,2,32,128]{3,2,1,0:T(8,128)S(1)}, u32[]{:S(2)}, u32[]{:S(2)}) collective-permute-start(f32[5,2,32,128]{3,2,1,0:T(8,128)S(1)} %get-tuple-element.13), channel_id=1, source_target_pairs={{0,16},{16,0},{32,48},{48,32},{64,80},{80,64},{96,112},{112,96},{1... | collective-permute-start | bytes 491528 | tf_op jit(solution)/shard_map/ppermute | solution.py:427
  9.2 4.2 %collective-permute-start.5 = (f32[3,32,128]{2,1,0:T(8,128)S(1)}, f32[3,32,128]{2,1,0:T(8,128)S(1)}, u32[]{:S(2)}, u32[]{:S(2)}) collective-permute-start(f32[3,32,128]{2,1,0:T(8,128)S(1)} %get-tuple-element.18), channel_id=1, source_target_pairs={{0,1},{1,2},{2,3},{3,0},{4,5},{5,6},{6,7},{7,4},{8,9},{9,10},{10,1... | collective-permute-start | bytes 147464 | tf_op jit(solution)/shard_map/ppermute | solution.py:431
  10.8 6.7 %collective-permute-start.4 = (f32[6,32,128]{2,1,0:T(8,128)S(1)}, f32[6,32,128]{2,1,0:T(8,128)S(1)}, u32[]{:S(2)}, u32[]{:S(2)}) collective-permute-start(f32[6,32,128]{2,1,0:T(8,128)S(1)} %get-tuple-element.17), channel_id=1, source_target_pairs={{0,3},{1,0},{2,1},{3,2},{4,7},{5,4},{6,5},{7,6},{8,11},{9,8},{10,9... | collective-permute-start | bytes 294920 | tf_op jit(solution)/shard_map/ppermute | solution.py:432
  11.3 6.2 %collective-permute-start.2 = (f32[5,2,16,128]{3,2,1,0:T(8,128)S(1)}, f32[5,2,16,128]{3,2,1,0:T(8,128)S(1)}, u32[]{:S(2)}, u32[]{:S(2)}) collective-permute-start(f32[5,2,16,128]{3,2,1,0:T(8,128)S(1)} %get-tuple-element.15), channel_id=1, source_target_pairs={{0,12},{4,8},{8,4},{12,0},{1,13},{5,9},{9,5},{13,1},{2,14},{6,10},... | collective-permute-start | bytes 245768 | tf_op jit(solution)/shard_map/ppermute | solution.py:429
  13.4 4.1 %collective-permute-start.3 = (f32[5,2,16,128]{3,2,1,0:T(8,128)S(1)}, f32[5,2,16,128]{3,2,1,0:T(8,128)S(1)}, u32[]{:S(2)}, u32[]{:S(2)}) collective-permute-start(f32[5,2,16,128]{3,2,1,0:T(8,128)S(1)} %get-tuple-element.16), channel_id=1, source_target_pairs={{0,4},{4,0},{8,12},{12,8},{1,5},{5,1},{9,13},{13,9},{2,6},{6,2},{1... | collective-permute-start | bytes 245768 | tf_op jit(solution)/shard_map/ppermute | solution.py:430
  17.9 14.2 %copy-start.4 = (f32[128,256]{1,0:T(8,128)S(1)}, f32[128,256]{1,0:T(8,128)}, u32[]{:S(2)}) copy-start(f32[128,256]{1,0:T(8,128)} %constant.2.clone.table) | copy-start | bytes 393220
  33.2 13.1 %all-to-all-start.1 = ((f32[16,2,8,128]{3,2,1,0:T(8,128)}), f32[16,2,8,128]{3,2,1,0:T(8,128)S(1)}, u32[]{:S(2)}, u32[]{:S(2)}) async-start(f32[16,2,8,128]{3,2,1,0:T(8,128)} %harmonics.1), calls=%async_computation.1 | async-start | bytes 262144 | tf_op jit(solution)/shard_map/all_to_all | solution.py:495

commit v6 on v4

--- a/solution.py
+++ b/solution.py
@@ -360,19 +360,14 @@
     lax.fori_loop(0, nt, step, 0)
 
 
-def harmonics_kernel(table, spread, out, held, sems):
+def harmonics_kernel(table, spread, out):
     sectors, parts, nt, nr = spread.shape
-    copies = []
     for p in range(parts):
         x = spread[:, p].reshape(sectors * nt, nr)
         y = jnp.dot(
             table[...], x, precision=lax.Precision.HIGHEST, preferred_element_type=jnp.float32
         )
-        held[p] = y.reshape(sectors, HARM // sectors, nr)
-        copies.append(pltpu.make_async_copy(held.at[p], out.at[:, p], sems.at[p]))
-        copies[p].start()
-    for copy in copies:
-        copy.wait()
+        out[:, p] = y.reshape(sectors, HARM // sectors, nr)
 
 
 def gather_kernel(parts, out):
@@ -476,15 +471,12 @@
         compiler_params=params,
         name="flow",
     )(mass_excess, speed_vector, thermal_excess, cells, *halos)
+    spread, new_rho = lax.optimization_barrier((spread, new_rho))
     terms = pl.pallas_call(
         harmonics_kernel,
         in_specs=[vmem] * 2,
-        out_specs=hbm,
+        out_specs=vmem,
         out_shape=sds((sectors, share, rows, nr), f32),
-        scratch_shapes=[
-            pltpu.VMEM((share, sectors, rows, nr), f32),
-            pltpu.SemaphoreType.DMA((share,)),
-        ],
         compiler_params=params,
         name="harmonics",
     )(table, spread)

time: 47.4 us -> 47.7 us (level)
  blocking collectives: 14.2 us -> 12.9 us
  Pallas kernels: 10.2 us -> 11.2 us
    all_to_all x1, blocking collectives: 14.2 us -> 12.9 us  [per_device(): terms = lax.all_to_all(terms, 'sector', 0, 0, tiled=True)]
    pallas_call x1, Pallas kernels: 5.32 us -> 6.28 us  [per_device(): pl.pallas_call(flow_kernel, in_specs=[vmem] * 10, out_shape=(sds((nt, na,...]
    pallas_call x1, Pallas kernels: 0.42 us -> 1.12 us  [per_device(): pl.pallas_call(temperature_kernel, in_specs=[vmem] * 9, out_specs=[vmem],...]
    pallas_call x1, Pallas kernels: 1.02 us -> 0.37 us  [per_device(): pl.pallas_call(harmonics_kernel, in_specs=[vmem] * 2, out_specs=vmem, out...]
  transfers between devices with their start and end apart: 7 -> 7, of which waited for: 4 -> 4; matrix products, arithmetic and copies ran while one was open for 0% -> 0% of each run, Pallas kernels for 14% -> 16%
where the time goes in v6:
time: 47.7 us; the launch traced here: 47.1 us
  starting transfers between devices  15.1 us (32%)
  blocking collectives  12.9 us (27%)
  Pallas kernels  11.2 us (23%)
  waiting for transfers between devices  6.86 us (14%)
  between operations  0.72 us (2%)
    all_to_all x1, blocking collectives, per_device(): terms = lax.all_to_all(terms, 'sector', 0, 0, tiled=True)  12.9 us
    pallas_call x1, Pallas kernels, per_device(): pl.pallas_call(flow_kernel, in_specs=[vmem] * 10, out_shape=(sds((nt, na,...  6.28 us
    ppermute x1, starting transfers between devices, per_device(): s_far = lax.ppermute(s_far, 'sector', pairs('sector', False))  5.97 us
    all_to_all x1, starting transfers between devices, per_device(): lax.all_to_all(cells.reshape(sectors, share, nt, nr), 'sector', 0, 0, til...  4.33 us
    all_to_all x1, waiting for transfers between devices, per_device(): lax.all_to_all(cells.reshape(sectors, share, nt, nr), 'sector', 0, 0, til...  3.63 us
    ppermute x1, starting transfers between devices, per_device(): a_far = lax.ppermute(a_far, 'ax', pairs('ax', False))  2.72 us
    ppermute x1, waiting for transfers between devices, per_device(): r_left = lax.ppermute(r_pack, 'rad', ring('rad', True))  1.82 us
    ppermute x1, starting transfers between devices, per_device(): r_left = lax.ppermute(r_pack, 'rad', ring('rad', True))  1.49 us
  transfers between devices with their start and end apart: 7, of which 4 were waited for; matrix products, arithmetic and copies ran while one was open for 0% of the time, Pallas kernels for 16%

profile of v6, /device:TPU:2, one launch (start us, length us, event | category | flops | bytes accessed | tf_op | source)
XLA Modules:
  0.0 47.1 jit_solution(11038912545055771057)
XLA Ops:
  0.7 1.1 %sector_edges.1 = (f32[5,2,32,128]{3,2,1,0:T(8,128)S(1)}, f32[5,2,32,128]{3,2,1,0:T(8,128)S(1)}) custom-call(f32[16,32,128]{2,1,0:T(8,128)} %rho.5, f32[3,16,32,128]{3,2,1,0:T(8,128)} %vel.9, f32[16,32,128]{2,1,0:T(8,128)} %temp.9), custom_call_target="tpu_custom_call" | custom-call | tf_op jit(solution)/shard_map/sector_edges/pallas_call | solution.py:388
  1.8 0.2 copy-done
  2.0 0.0 copy-done.1
  2.1 0.4 tile_edges.1
  2.5 2.7 %collective-permute-start.2 = (f32[5,2,16,128]{3,2,1,0:T(8,128)S(1)}, f32[5,2,16,128]{3,2,1,0:T(8,128)S(1)}, u32[]{:S(2)}, u32[]{:S(2)}) collective-permute-start(f32[5,2,16,128]{3,2,1,0:T(8,128)S(1)} %get-tuple-element.16), channel_id=1, source_target_pairs={{0,12},{4,8},{8,4},{12,0},{1,13},{5,9},{9,5},{13,1},{2,14},{6,10},... | collective-permute-start | bytes 245768 | tf_op jit(solution)/shard_map/ppermute | solution.py:420
  5.2 6.0 %collective-permute-start.1 = (f32[5,2,32,128]{3,2,1,0:T(8,128)S(1)}, f32[5,2,32,128]{3,2,1,0:T(8,128)S(1)}, u32[]{:S(2)}, u32[]{:S(2)}) collective-permute-start(f32[5,2,32,128]{3,2,1,0:T(8,128)S(1)} %get-tuple-element.15.after), channel_id=1, source_target_pairs={{0,240},{16,32},{32,16},{48,64},{64,48},{80,96},{96,80},{112,128},... | collective-permute-start | bytes 491528 | tf_op jit(solution)/shard_map/ppermute | solution.py:419
  11.2 0.0 collective-permute-start
  11.2 1.5 %collective-permute-start.4 = (f32[6,32,128]{2,1,0:T(8,128)S(1)}, f32[6,32,128]{2,1,0:T(8,128)S(1)}, u32[]{:S(2)}, u32[]{:S(2)}) collective-permute-start(f32[6,32,128]{2,1,0:T(8,128)S(1)} %get-tuple-element.18), channel_id=1, source_target_pairs={{0,1},{1,2},{2,3},{3,0},{4,5},{5,6},{6,7},{7,4},{8,9},{9,10},{10,1... | collective-permute-start | bytes 294920 | tf_op jit(solution)/shard_map/ppermute | solution.py:422
  12.7 0.5 %collective-permute-start.5 = (f32[6,32,128]{2,1,0:T(8,128)S(1)}, f32[6,32,128]{2,1,0:T(8,128)S(1)}, u32[]{:S(2)}, u32[]{:S(2)}) collective-permute-start(f32[6,32,128]{2,1,0:T(8,128)S(1)} %get-tuple-element.18), channel_id=1, source_target_pairs={{0,3},{1,0},{2,1},{3,2},{4,7},{5,4},{6,5},{7,6},{8,11},{9,8},{10,9... | collective-permute-start | bytes 294920 | tf_op jit(solution)/shard_map/ppermute | solution.py:423
  13.2 0.0 collective-permute-done.2.a_far
  13.2 0.0 collective-permute-start.3
  13.2 1.3 %inner.1.base = f32[16,32,128]{2,1,0:T(8,128)S(1)} custom-call(f32[3,16,32,128]{3,2,1,0:T(8,128)S(1)} %copy-done, f32[16,32,128]{2,1,0:T(8,128)S(1)} %copy-done.1, f32[16,32,128]{2,1,0:T(8,128)S(1)} %copy-done.3), custom_call_target="tpu_custom_call" | custom-call | flops 5242880 | bytes 1572864 | tf_op jit(solution)/shard_map/inner/pallas_call | solution.py:425
  14.5 0.0 collective-permute-done.3.a_near
  14.5 1.8 %collective-permute-done.4.r_left = f32[6,32,128]{2,1,0:T(8,128)S(1)} collective-permute-done((f32[6,32,128]{2,1,0:T(8,128)S(1)}, f32[6,32,128]{2,1,0:T(8,128)S(1)}, u32[]{:S(2)}, u32[]{:S(2)}) %collective-permute-start.4) | collective-permute-done | bytes 98336 | tf_op jit(solution)/shard_map/ppermute | solution.py:422
  16.3 1.2 %collective-permute-done.5.r_right = f32[6,32,128]{2,1,0:T(8,128)S(1)} collective-permute-done((f32[6,32,128]{2,1,0:T(8,128)S(1)}, f32[6,32,128]{2,1,0:T(8,128)S(1)}, u32[]{:S(2)}, u32[]{:S(2)}) %collective-permute-start.5) | collective-permute-done | bytes 98336 | tf_op jit(solution)/shard_map/ppermute | solution.py:423
  17.5 0.2 collective-permute-done.s_near
  17.7 1.1 %temperature.1.cells = f32[32,16,128]{2,1,0:T(8,128)} custom-call(f32[3,16,32,128]{3,2,1,0:T(8,128)S(1)} %copy-done, f32[16,32,128]{2,1,0:T(8,128)S(1)} %copy-done.1, f32[16,32,128]{2,1,0:T(8,128)S(1)} %inner.1.base, f32[5,2,32,128]{3,2,1,0:T(8,128)S(1)} %collective-permute-done.s_near, f32[5,2,32,128]{3,2,1,0:T(8,128)S(1)} %collective-permute-done.1.s_far, ...), custom_call_target="tpu_custom_call" | custom-call | tf_op jit(solution)/shard_map/temperature/pallas_call | solution.py:437
  18.8 4.3 %all-to-all-start = ((f32[16,2,16,128]{3,2,1,0:T(8,128)}), f32[16,2,16,128]{3,2,1,0:T(8,128)S(1)}, u32[]{:S(2)}, u32[]{:S(2)}) async-start(f32[16,2,16,128]{3,2,1,0:T(8,128)} %bitcast), calls=%async_computation | async-start | bytes 524288 | tf_op jit(solution)/shard_map/all_to_all | solution.py:449
  23.2 0.0 copy-start.4
  23.2 6.3 %flow.1 = (f32[16,32,128]{2,1,0:T(8,128)}, f32[3,16,32,128]{3,2,1,0:T(8,128)}, f32[16,32,128]{2,1,0:T(8,128)}) custom-call(f32[16,32,128]{2,1,0:T(8,128)S(1)} %copy-done.2, f32[3,16,32,128]{3,2,1,0:T(8,128)S(1)} %copy-done, f32[16,32,128]{2,1,0:T(8,128)S(1)} %copy-done.1, f32[32,16,128]{2,1,0:T(8,128)} %temperature.1.cells, ...), custom_call_target="tpu_custom_call" | custom-call | flops 11796480 | bytes 2883584 | tf_op jit(solution)/shard_map/flow/pallas_call | solution.py:452
  29.5 3.6 %all-to-all-done.spread = f32[16,2,16,128]{3,2,1,0:T(8,128)S(1)} async-done(((f32[16,2,16,128]{3,2,1,0:T(8,128)}), f32[16,2,16,128]{3,2,1,0:T(8,128)S(1)}, u32[]{:S(2)}, u32[]{:S(2)}) %all-to-all-start) | async-done | bytes 262176 | tf_op jit(solution)/shard_map/all_to_all | solution.py:449
  33.1 0.4 harmonics.1
  33.5 12.9 %all_to_all.10 = f32[16,2,8,128]{3,2,1,0:T(8,128)S(1)} all-to-all(f32[16,2,8,128]{3,2,1,0:T(8,128)S(1)} %harmonics.1), channel_id=1, replica_groups=mesh['sector'=16,'ax'=4,'rad'=4] {'sector'}, dimensions={0} | all-to-all | bytes 262144 | tf_op jit(solution)/shard_map/all_to_all | solution.py:483
  46.4 0.7 %gather.1 = f32[8,32,128]{2,1,0:T(8,128)} custom-call(f32[32,8,128]{2,1,0:T(8,128)S(1)} %bitcast.2), custom_call_target="tpu_custom_call" | custom-call | tf_op jit(solution)/shard_map/gather/pallas_call | solution.py:484
  (8 shorter events, 0.0 us)
Async XLA Ops:
  0.6 1.1 %copy-start.2 = (f32[16,32,128]{2,1,0:T(8,128)S(1)}, f32[16,32,128]{2,1,0:T(8,128)}, u32[]{:S(2)}) copy-start(f32[16,32,128]{2,1,0:T(8,128)} %rho.5) | copy-start | bytes 786436
  0.6 1.4 %copy-start = (f32[3,16,32,128]{3,2,1,0:T(8,128)S(1)}, f32[3,16,32,128]{3,2,1,0:T(8,128)}, u32[]{:S(2)}) copy-start(f32[3,16,32,128]{3,2,1,0:T(8,128)} %vel.9) | copy-start | bytes 2359300
  0.7 1.4 %copy-start.1 = (f32[16,32,128]{2,1,0:T(8,128)S(1)}, f32[16,32,128]{2,1,0:T(8,128)}, u32[]{:S(2)}) copy-start(f32[16,32,128]{2,1,0:T(8,128)} %temp.9) | copy-start | bytes 786436
  2.1 11.2 %copy-start.3 = (f32[16,32,128]{2,1,0:T(8,128)S(1)}, f32[16,32,128]{2,1,0:T(8,128)}, u32[]{:S(2)}) copy-start(f32[16,32,128]{2,1,0:T(8,128)} %heat.1) | copy-start | bytes 786436
  2.5 10.7 %collective-permute-start.2 = (f32[5,2,16,128]{3,2,1,0:T(8,128)S(1)}, f32[5,2,16,128]{3,2,1,0:T(8,128)S(1)}, u32[]{:S(2)}, u32[]{:S(2)}) collective-permute-start(f32[5,2,16,128]{3,2,1,0:T(8,128)S(1)} %get-tuple-element.16), channel_id=1, source_target_pairs={{0,12},{4,8},{8,4},{12,0},{1,13},{5,9},{9,5},{13,1},{2,14},{6,10},... | collective-permute-start | bytes 245768 | tf_op jit(solution)/shard_map/ppermute | solution.py:420
  5.2 12.3 %collective-permute-start.1 = (f32[5,2,32,128]{3,2,1,0:T(8,128)S(1)}, f32[5,2,32,128]{3,2,1,0:T(8,128)S(1)}, u32[]{:S(2)}, u32[]{:S(2)}) collective-permute-start(f32[5,2,32,128]{3,2,1,0:T(8,128)S(1)} %get-tuple-element.15.after), channel_id=1, source_target_pairs={{0,240},{16,32},{32,16},{48,64},{64,48},{80,96},{96,80},{112,128},... | collective-permute-start | bytes 491528 | tf_op jit(solution)/shard_map/ppermute | solution.py:419
  11.2 6.5 %collective-permute-start = (f32[5,2,32,128]{3,2,1,0:T(8,128)S(1)}, f32[5,2,32,128]{3,2,1,0:T(8,128)S(1)}, u32[]{:S(2)}, u32[]{:S(2)}) collective-permute-start(f32[5,2,32,128]{3,2,1,0:T(8,128)S(1)} %get-tuple-element.14), channel_id=1, source_target_pairs={{0,16},{16,0},{32,48},{48,32},{64,80},{80,64},{96,112},{112,96},{1... | collective-permute-start | bytes 491528 | tf_op jit(solution)/shard_map/ppermute | solution.py:418
  11.2 5.1 %collective-permute-start.4 = (f32[6,32,128]{2,1,0:T(8,128)S(1)}, f32[6,32,128]{2,1,0:T(8,128)S(1)}, u32[]{:S(2)}, u32[]{:S(2)}) collective-permute-start(f32[6,32,128]{2,1,0:T(8,128)S(1)} %get-tuple-element.18), channel_id=1, source_target_pairs={{0,1},{1,2},{2,3},{3,0},{4,5},{5,6},{6,7},{7,4},{8,9},{9,10},{10,1... | collective-permute-start | bytes 294920 | tf_op jit(solution)/shard_map/ppermute | solution.py:422
  12.7 4.8 %collective-permute-start.5 = (f32[6,32,128]{2,1,0:T(8,128)S(1)}, f32[6,32,128]{2,1,0:T(8,128)S(1)}, u32[]{:S(2)}, u32[]{:S(2)}) collective-permute-start(f32[6,32,128]{2,1,0:T(8,128)S(1)} %get-tuple-element.18), channel_id=1, source_target_pairs={{0,3},{1,0},{2,1},{3,2},{4,7},{5,4},{6,5},{7,6},{8,11},{9,8},{10,9... | collective-permute-start | bytes 294920 | tf_op jit(solution)/shard_map/ppermute | solution.py:423
  13.2 1.3 %collective-permute-start.3 = (f32[5,2,16,128]{3,2,1,0:T(8,128)S(1)}, f32[5,2,16,128]{3,2,1,0:T(8,128)S(1)}, u32[]{:S(2)}, u32[]{:S(2)}) collective-permute-start(f32[5,2,16,128]{3,2,1,0:T(8,128)S(1)} %get-tuple-element.17), channel_id=1, source_target_pairs={{0,4},{4,0},{8,12},{12,8},{1,5},{5,1},{9,13},{13,9},{2,6},{6,2},{1... | collective-permute-start | bytes 245768 | tf_op jit(solution)/shard_map/ppermute | solution.py:421
  18.8 14.3 %all-to-all-start = ((f32[16,2,16,128]{3,2,1,0:T(8,128)}), f32[16,2,16,128]{3,2,1,0:T(8,128)S(1)}, u32[]{:S(2)}, u32[]{:S(2)}) async-start(f32[16,2,16,128]{3,2,1,0:T(8,128)} %bitcast), calls=%async_computation | async-start | bytes 524288 | tf_op jit(solution)/shard_map/all_to_all | solution.py:449
  23.2 9.9 %copy-start.4 = (f32[128,256]{1,0:T(8,128)S(1)}, f32[128,256]{1,0:T(8,128)}, u32[]{:S(2)}) copy-start(f32[128,256]{1,0:T(8,128)} %constant.2.clone.table) | copy-start | bytes 393220
